TPU v7x, 256 devices: a whole 4x4x8 slice. The times are simulated.
256 devices in a mesh: section: 2 (over z_lo), dp: 8 (over z_hi, core), tensor: 16 (over x, y).
Axes of the slice: x: 4, y: 4, z: 8 (z_hi: 4, z_lo: 2; z = z_hi * 2 + z_lo), core: 2. Of those that a mesh axis runs over, the one named last changes fastest.
Arguments:
- tokens: bfloat16 [4, 128, 8192], P(None, None, 'dp'), may hold values from -6 to 6
- w_in: bfloat16 [2, 8192, 14336], P('section', 'dp', 'tensor'), may hold values from -2 to 2
- w_out: bfloat16 [2, 14336, 8192], P('section', 'tensor', 'dp'), may hold values from -0.046875 to 0.046875
- cotangent: bfloat16 [4, 128, 8192], P(None, None, 'dp'), may hold values from -6 to 6
Outputs:
- section_out: bfloat16 [2, 4, 128, 8192], P('section', None, None, 'dp')
- input_grad: bfloat16 [2, 4, 128, 8192], P('section', None, None, 'dp')
- w_in_grad: bfloat16 [2, 8192, 14336], P('section', 'dp', 'tensor')
- w_out_grad: bfloat16 [2, 14336, 8192], P('section', 'tensor', 'dp')
All inputs are finite; a program needn't handle non-finite values.
Results may differ from a plain program's by a relative error of at most 0.013.
The roundings to bfloat16 on the way count: a program that leaves them out, or rounds other values in their place, can miss the bound.
Values may be sent and summed in bfloat16 or wider, within the bound.
No kernel may reach another device: no remote copies, remote signals or barrier semaphores. Data moves between devices by JAX's collectives and lax.ppermute only.
A program may use at most 128 MiB of HBM per device.

v0:
```python
import jax
import jax.numpy as jnp
from jax import lax
from jax.sharding import PartitionSpec as P

D = 8192


root_two_pi = 0.7978845608


def passed_along(block, axis, distance):
    devices = range(lax.axis_size(axis))
    route = [(i - distance, i) for i in devices if i - distance in devices]
    return lax.ppermute(block, axis, route)


def gelu_value(pre_act):
    inner = jnp.tanh(root_two_pi * (pre_act + 0.044715 * pre_act**3))
    return 0.5 * pre_act * (1.0 + inner)


def gelu_slope(pre_act):
    inner = jnp.tanh(root_two_pi * (pre_act + 0.044715 * pre_act**3))
    return 0.5 * (1.0 + inner) + 0.5 * pre_act * (1.0 - inner * inner) * root_two_pi * (
        1.0 + 3.0 * 0.044715 * pre_act * pre_act
    )


def section_forward(section_input, weight_in, weight_out):
    values = section_input.astype(jnp.float32)
    total, squares = lax.psum((jnp.sum(values, 1), jnp.sum(values * values, 1)), "dp")
    row_mean = total / D
    inv_scale = lax.rsqrt(squares / D - row_mean * row_mean + 1e-05)
    normed_bf = ((values - row_mean[:, None]) * inv_scale[:, None]).astype(jnp.bfloat16)
    pre_share = lax.psum_scatter(
        jnp.dot(normed_bf, weight_in, preferred_element_type=jnp.float32),
        "dp",
        scatter_dimension=0,
        tiled=True,
    )
    hidden = lax.all_gather(gelu_value(pre_share).astype(jnp.bfloat16), "dp", axis=0, tiled=True)
    branch = lax.psum(jnp.dot(hidden, weight_out, preferred_element_type=jnp.float32), "tensor")
    output = (values + branch).astype(jnp.bfloat16)
    return (output, section_input, row_mean, inv_scale, normed_bf, pre_share, hidden)


def finish_rows(grad_rows, grad_normed, input_rows, mean_rows, scale_rows):
    normed = (input_rows.astype(jnp.float32) - mean_rows[:, None]) * scale_rows[:, None]
    first_sum, second_sum = lax.psum(
        (jnp.sum(grad_normed, 1), jnp.sum(grad_normed * normed, 1)), "dp"
    )
    result = grad_rows.astype(jnp.float32) + scale_rows[:, None] * (
        grad_normed - first_sum[:, None] / D - normed * second_sum[:, None] / D
    )
    return result.astype(jnp.bfloat16)


def section_backward(grad_out, record, weight_in, weight_out):
    output, section_input, row_mean, inv_scale, normed_bf, pre_share, hidden = record
    contract_last = (((1,), (1,)), ((), ()))
    contract_first = (((0,), (0,)), ((), ()))
    grad_share = lax.psum_scatter(
        lax.dot_general(grad_out, weight_out, contract_last, preferred_element_type=jnp.float32),
        "dp",
        scatter_dimension=0,
        tiled=True,
    )
    grad_pre = lax.all_gather(
        (grad_share * gelu_slope(pre_share)).astype(jnp.bfloat16), "dp", axis=0, tiled=True
    )
    grad_w_out = lax.dot_general(
        hidden, grad_out, contract_first, preferred_element_type=jnp.float32
    )
    grad_w_in = lax.dot_general(
        normed_bf, grad_pre, contract_first, preferred_element_type=jnp.float32
    )
    grad_normed = lax.psum(
        lax.dot_general(grad_pre, weight_in, contract_last, preferred_element_type=jnp.float32),
        "tensor",
    )
    grad_in = finish_rows(grad_out, grad_normed, section_input, row_mean, inv_scale)
    return (grad_in, grad_w_in, grad_w_out)


def select_record(first_section, early_record, later_record):
    return tuple(
        (
            jnp.where(first_section, early_part, later_part)
            for early_part, later_part in zip(early_record, later_record)
        )
    )


def body(tokens, w_in, w_out, cotangent):
    first_section = lax.axis_index("section") == 0
    weight_in = w_in[0]
    weight_out = w_out[0]
    micro_count = tokens.shape[0]
    records = []
    arrived = jnp.zeros(tokens.shape[1:], jnp.bfloat16)
    for tick_no in range(micro_count + 1):
        section_input = jnp.where(first_section, tokens[min(tick_no, micro_count - 1)], arrived)
        record = section_forward(section_input, weight_in, weight_out)
        records.append(record)
        if tick_no < micro_count:
            arrived = passed_along(record[0], "section", 1)
    total_in = jnp.zeros(weight_in.shape, jnp.float32)
    total_out = jnp.zeros(weight_out.shape, jnp.float32)
    arrived_grad = jnp.zeros(tokens.shape[1:], jnp.bfloat16)
    input_grads = []
    for tick_no in range(micro_count + 1):
        record = select_record(
            first_section, records[max(tick_no - 1, 0)], records[min(tick_no + 1, micro_count)]
        )
        grad_out = jnp.where(first_section, arrived_grad, cotangent[min(tick_no, micro_count - 1)])
        grad_in, grad_w_in, grad_w_out = section_backward(grad_out, record, weight_in, weight_out)
        valid_tick = jnp.where(first_section, float(tick_no >= 1), float(tick_no < micro_count))
        total_in = total_in + valid_tick * grad_w_in
        total_out = total_out + valid_tick * grad_w_out
        input_grads.append(grad_in)
        if tick_no < micro_count:
            arrived_grad = passed_along(grad_in, "section", -1)
    section_out = jnp.stack(
        [
            jnp.where(first_section, records[batch_no][0], records[batch_no + 1][0])
            for batch_no in range(micro_count)
        ]
    )[None]
    input_grad = jnp.stack(
        [
            jnp.where(first_section, input_grads[batch_no + 1], input_grads[batch_no])
            for batch_no in range(micro_count)
        ]
    )[None]
    return (
        section_out,
        input_grad,
        total_in.astype(jnp.bfloat16)[None],
        total_out.astype(jnp.bfloat16)[None],
    )


def solution(mesh):
    in_specs = (
        P(None, None, "dp"),
        P("section", "dp", "tensor"),
        P("section", "tensor", "dp"),
        P(None, None, "dp"),
    )
    out_specs = (
        P("section", None, None, "dp"),
        P("section", None, None, "dp"),
        P("section", "dp", "tensor"),
        P("section", "tensor", "dp"),
    )
    return jax.shard_map(body, mesh=mesh, in_specs=in_specs, out_specs=out_specs, check_vma=False)
```

profile of v0, /device:TPU:1, one launch (start us, length us, event | category | flops | bytes accessed | tf_op | source)
XLA Modules:
  0.0 1292.8 jit_solution(11618955899203527345)
XLA Ops:
  8.5 17.6 %all-reduce.10 = (f32[128]{0:T(128)S(1)}, f32[128]{0:T(128)S(1)}) all-reduce(f32[128]{0:T(128)S(1)} %get-tuple-element.5, f32[128]{0:T(128)S(1)} %get-tuple-element.4), channel_id=1, replica_groups=mesh['section'=2,'dp'=8,'tensor'=16] {'dp'}, use_global_device_ids=true, to_apply=%region_3.4 | all-reduce | flops 256 | bytes 2048 | tf_op jit(solution)/shard_map/psum | solution.py:32
  29.1 36.2 %reduce-scatter.11.cloned.1.call-done = f32[16,896]{1,0:T(8,128)} async-done(((f32[128,896]{1,0:T(8,128)}), f32[16,896]{1,0:T(8,128)}) %reduce-scatter.11.cloned.1.call-update) | async-done | bytes 57360 | tf_op jit(solution)/shard_map/reduce_scatter | solution.py:36
  66.1 17.3 %all_gather.30 = bf16[128,896]{1,0:T(8,128)(2,1)S(1)} all-gather(bf16[16,896]{1,0:T(8,128)(2,1)S(1)} %fusion.108), channel_id=1, replica_groups=mesh['section'=2,'dp'=8,'tensor'=16] {'dp'}, dimensions={0}, use_global_device_ids=true | all-gather | bytes 258048 | tf_op jit(solution)/shard_map/all_gather | solution.py:42
  85.4 91.5 %all-reduce.18.cloned.1.call-done = f32[128,1024]{1,0:T(8,128)} async-done(((f32[128,1024]{1,0:T(8,128)}), f32[128,1024]{1,0:T(8,128)}) %all-reduce.18.cloned.1.call-update) | async-done | bytes 524304 | tf_op jit(solution)/shard_map/psum | solution.py:43
  219.8 38.6 %reduce-scatter.13.cloned.1.call-done = f32[16,896]{1,0:T(8,128)} async-done(((f32[128,896]{1,0:T(8,128)}), f32[16,896]{1,0:T(8,128)}) %reduce-scatter.13.cloned.1.call-update) | async-done | bytes 57360 | tf_op jit(solution)/shard_map/reduce_scatter | solution.py:36
  259.4 16.9 %all_gather.35 = bf16[128,896]{1,0:T(8,128)(2,1)S(1)} all-gather(bf16[16,896]{1,0:T(8,128)(2,1)S(1)} %get-tuple-element.90), channel_id=1, replica_groups=mesh['section'=2,'dp'=8,'tensor'=16] {'dp'}, dimensions={0}, use_global_device_ids=true | all-gather | bytes 258048 | tf_op jit(solution)/shard_map/all_gather | solution.py:69
  293.9 93.3 %all-reduce.28.cloned.1.call-done = (f32[128,1024]{1,0:T(8,128)}, f32[128,1024]{1,0:T(8,128)}) async-done(((f32[128,1024]{1,0:T(8,128)}, f32[128,1024]{1,0:T(8,128)}), (f32[128,1024]{1,0:T(8,128)}, f32[128,1024]{1,0:T(8,128)})) %all-reduce.28.cloned.1.call-update) | async-done | bytes 1048592 | tf_op jit(solution)/shard_map/psum | solution.py:43
  395.9 16.8 %all-reduce.8 = (f32[128]{0:T(128)S(1)}, f32[128]{0:T(128)S(1)}, f32[128]{0:T(128)S(1)}, f32[128]{0:T(128)S(1)}) all-reduce(f32[128]{0:T(128)S(1)} %get-tuple-element.79, f32[128]{0:T(128)S(1)} %get-tuple-element.80, f32[128]{0:T(128)S(1)} %get-tuple-element.15, ...), channel_id=1, replica_groups=mesh['section'=2,'dp'=8,'tensor'=16] {'dp'}, use_global_device_ids=true, to_apply=%region_15.16 | all-reduce | flops 512 | bytes 4096 | tf_op jit(solution)/shard_map/psum | solution.py:32
  428.8 21.8 %reduce-scatter.15.cloned.1.call-done = f32[16,896]{1,0:T(8,128)} async-done(((f32[128,896]{1,0:T(8,128)}), f32[16,896]{1,0:T(8,128)}) %reduce-scatter.15.cloned.1.call-update) | async-done | bytes 57360 | tf_op jit(solution)/shard_map/reduce_scatter | solution.py:36
  450.5 38.8 %reduce-scatter.23.cloned.1.call-done = f32[16,896]{1,0:T(8,128)} async-done(((f32[128,896]{1,0:T(8,128)}), f32[16,896]{1,0:T(8,128)}) %reduce-scatter.23.cloned.1.call-update) | async-done | bytes 57360 | tf_op jit(solution)/shard_map/reduce_scatter | solution.py:63
  490.3 17.0 %all_gather.36 = bf16[128,896]{1,0:T(8,128)(2,1)S(1)} all-gather(bf16[16,896]{1,0:T(8,128)(2,1)S(1)} %get-tuple-element.88), channel_id=1, replica_groups=mesh['section'=2,'dp'=8,'tensor'=16] {'dp'}, dimensions={0}, use_global_device_ids=true | all-gather | bytes 258048 | tf_op jit(solution)/shard_map/all_gather | solution.py:69
  524.8 93.5 %all-reduce.26.cloned.1.call-done = (f32[128,1024]{1,0:T(8,128)}, f32[128,1024]{1,0:T(8,128)}) async-done(((f32[128,1024]{1,0:T(8,128)}, f32[128,1024]{1,0:T(8,128)}), (f32[128,1024]{1,0:T(8,128)}, f32[128,1024]{1,0:T(8,128)})) %all-reduce.26.cloned.1.call-update) | async-done | bytes 1048592 | tf_op jit(solution)/shard_map/psum | solution.py:43
  628.1 16.9 %all-reduce.7 = (f32[128]{0:T(128)S(1)}, f32[128]{0:T(128)S(1)}, f32[128]{0:T(128)S(1)}, f32[128]{0:T(128)S(1)}) all-reduce(f32[128]{0:T(128)S(1)} %get-tuple-element.76, f32[128]{0:T(128)S(1)} %get-tuple-element.77, f32[128]{0:T(128)S(1)} %get-tuple-element.13, ...), channel_id=1, replica_groups=mesh['section'=2,'dp'=8,'tensor'=16] {'dp'}, use_global_device_ids=true, to_apply=%region_21.22 | all-reduce | flops 512 | bytes 4096 | tf_op jit(solution)/shard_map/psum | solution.py:32
  662.0 20.9 %reduce-scatter.17.cloned.1.call-done = f32[16,896]{1,0:T(8,128)} async-done(((f32[128,896]{1,0:T(8,128)}), f32[16,896]{1,0:T(8,128)}) %reduce-scatter.17.cloned.1.call-update) | async-done | bytes 57360 | tf_op jit(solution)/shard_map/reduce_scatter | solution.py:36
  682.9 38.6 %reduce-scatter.25.cloned.1.call-done = f32[16,896]{1,0:T(8,128)} async-done(((f32[128,896]{1,0:T(8,128)}), f32[16,896]{1,0:T(8,128)}) %reduce-scatter.25.cloned.1.call-update) | async-done | bytes 57360 | tf_op jit(solution)/shard_map/reduce_scatter | solution.py:63
  722.5 17.4 %all_gather.37 = bf16[128,896]{1,0:T(8,128)(2,1)S(1)} all-gather(bf16[16,896]{1,0:T(8,128)(2,1)S(1)} %get-tuple-element.86), channel_id=1, replica_groups=mesh['section'=2,'dp'=8,'tensor'=16] {'dp'}, dimensions={0}, use_global_device_ids=true | all-gather | bytes 258048 | tf_op jit(solution)/shard_map/all_gather | solution.py:69
  757.5 93.4 %all-reduce.24.cloned.1.call-done = (f32[128,1024]{1,0:T(8,128)}, f32[128,1024]{1,0:T(8,128)}) async-done(((f32[128,1024]{1,0:T(8,128)}, f32[128,1024]{1,0:T(8,128)}), (f32[128,1024]{1,0:T(8,128)}, f32[128,1024]{1,0:T(8,128)})) %all-reduce.24.cloned.1.call-update) | async-done | bytes 1048592 | tf_op jit(solution)/shard_map/psum | solution.py:43
  860.5 16.8 %all-reduce.6 = (f32[128]{0:T(128)S(1)}, f32[128]{0:T(128)S(1)}, f32[128]{0:T(128)S(1)}, f32[128]{0:T(128)S(1)}) all-reduce(f32[128]{0:T(128)S(1)} %get-tuple-element.17, f32[128]{0:T(128)S(1)} %get-tuple-element.16, f32[128]{0:T(128)S(1)} %get-tuple-element.11, ...), channel_id=1, replica_groups=mesh['section'=2,'dp'=8,'tensor'=16] {'dp'}, use_global_device_ids=true, to_apply=%region_27.28 | all-reduce | flops 512 | bytes 4096 | tf_op jit(solution)/shard_map/psum | solution.py:32
  915.0 38.8 %reduce-scatter.27.cloned.1.call-done = f32[16,896]{1,0:T(8,128)} async-done(((f32[128,896]{1,0:T(8,128)}), f32[16,896]{1,0:T(8,128)}) %reduce-scatter.27.cloned.1.call-update) | async-done | bytes 57360 | tf_op jit(solution)/shard_map/reduce_scatter | solution.py:63
  954.7 16.9 %all_gather.38 = bf16[128,896]{1,0:T(8,128)(2,1)S(1)} all-gather(bf16[16,896]{1,0:T(8,128)(2,1)S(1)} %fusion.172), channel_id=1, replica_groups=mesh['section'=2,'dp'=8,'tensor'=16] {'dp'}, dimensions={0}, use_global_device_ids=true | all-gather | bytes 258048 | tf_op jit(solution)/shard_map/all_gather | solution.py:69
  979.1 88.0 %all-reduce.20.cloned.1.call-done = f32[128,1024]{1,0:T(8,128)} async-done(((f32[128,1024]{1,0:T(8,128)}), f32[128,1024]{1,0:T(8,128)}) %all-reduce.20.cloned.1.call-update) | async-done | bytes 524304 | tf_op jit(solution)/shard_map/psum | solution.py:78
  1105.0 28.8 %reduce-scatter.29.cloned.1.call-done = f32[16,896]{1,0:T(8,128)} async-done(((f32[128,896]{1,0:T(8,128)}), f32[16,896]{1,0:T(8,128)}) %reduce-scatter.29.cloned.1.call-update) | async-done | bytes 57360 | tf_op jit(solution)/shard_map/reduce_scatter | solution.py:63
  1134.7 17.1 %all_gather.34 = bf16[128,896]{1,0:T(8,128)(2,1)S(1)} all-gather(bf16[16,896]{1,0:T(8,128)(2,1)S(1)} %get-tuple-element.85), channel_id=1, replica_groups=mesh['section'=2,'dp'=8,'tensor'=16] {'dp'}, dimensions={0}, use_global_device_ids=true | all-gather | bytes 258048 | tf_op jit(solution)/shard_map/all_gather | solution.py:42
  1184.6 80.7 %all-reduce.22.cloned.1.call-done = (f32[128,1024]{1,0:T(8,128)}, f32[128,1024]{1,0:T(8,128)}) async-done(((f32[128,1024]{1,0:T(8,128)}, f32[128,1024]{1,0:T(8,128)}), (f32[128,1024]{1,0:T(8,128)}, f32[128,1024]{1,0:T(8,128)})) %all-reduce.22.cloned.1.call-update) | async-done | bytes 1048592 | tf_op jit(solution)/shard_map/psum | solution.py:43
  (228 shorter events, 304.8 us)
Async XLA Ops:
  7.2 58.1 %reduce-scatter.11.cloned.1.call-start = ((), (), s32[]{:S(2)}) async-start(), calls=%async_computation.10 | async-start | bytes 516096 | tf_op jit(solution)/shard_map/reduce_scatter | solution.py:36
  29.0 147.9 %all-reduce.18.cloned.1.call-start = ((), (), s32[]{:S(2)}) async-start(), calls=%async_computation.11 | async-start | bytes 1048576 | tf_op jit(solution)/shard_map/psum | solution.py:43
  85.4 134.4 %reduce-scatter.21.cloned.1.call-start = ((), (), s32[]{:S(2)}) async-start(), calls=%async_computation.16 | async-start | bytes 516096 | tf_op jit(solution)/shard_map/reduce_scatter | solution.py:63
  178.1 6.8 collective-permute-start
  183.7 74.6 %reduce-scatter.13.cloned.1.call-start = ((), (), s32[]{:S(2)}) async-start(), calls=%async_computation.12 | async-start | bytes 516096 | tf_op jit(solution)/shard_map/reduce_scatter | solution.py:36
  204.3 182.8 %all-reduce.28.cloned.1.call-start = ((), (), s32[]{:S(2)}) async-start(), calls=%async_computation.25 | async-start | bytes 2097152 | tf_op jit(solution)/shard_map/psum | solution.py:43
  293.8 156.7 %reduce-scatter.15.cloned.1.call-start = ((), (), s32[]{:S(2)}) async-start(), calls=%async_computation.13 | async-start | bytes 516096 | tf_op jit(solution)/shard_map/reduce_scatter | solution.py:36
  389.2 6.4 collective-permute-start.1
  415.5 73.8 %reduce-scatter.23.cloned.1.call-start = ((), (), s32[]{:S(2)}) async-start(), calls=%async_computation.17 | async-start | bytes 516096 | tf_op jit(solution)/shard_map/reduce_scatter | solution.py:63
  417.0 9.2 collective-permute-start.4
  428.7 189.6 %all-reduce.26.cloned.1.call-start = ((), (), s32[]{:S(2)}) async-start(), calls=%async_computation.24 | async-start | bytes 2097152 | tf_op jit(solution)/shard_map/psum | solution.py:43
  524.8 158.1 %reduce-scatter.17.cloned.1.call-start = ((), (), s32[]{:S(2)}) async-start(), calls=%async_computation.14 | async-start | bytes 516096 | tf_op jit(solution)/shard_map/reduce_scatter | solution.py:36
  620.3 6.5 collective-permute-start.2
  647.9 73.6 %reduce-scatter.25.cloned.1.call-start = ((), (), s32[]{:S(2)}) async-start(), calls=%async_computation.18 | async-start | bytes 516096 | tf_op jit(solution)/shard_map/reduce_scatter | solution.py:63
  650.1 9.3 collective-permute-start.5
  661.9 188.9 %all-reduce.24.cloned.1.call-start = ((), (), s32[]{:S(2)}) async-start(), calls=%async_computation.23 | async-start | bytes 2097152 | tf_op jit(solution)/shard_map/psum | solution.py:43
  757.5 157.5 %reduce-scatter.19.cloned.1.call-start = ((), (), s32[]{:S(2)}) async-start(), calls=%async_computation.15 | async-start | bytes 516096 | tf_op jit(solution)/shard_map/reduce_scatter | solution.py:36
  852.9 6.4 collective-permute-start.3
  880.0 73.8 %reduce-scatter.27.cloned.1.call-start = ((), (), s32[]{:S(2)}) async-start(), calls=%async_computation.19 | async-start | bytes 516096 | tf_op jit(solution)/shard_map/reduce_scatter | solution.py:63
  882.2 9.4 collective-permute-start.6
  894.8 172.3 %all-reduce.20.cloned.1.call-start = ((), (), s32[]{:S(2)}) async-start(), calls=%async_computation.20 | async-start | bytes 1048576 | tf_op jit(solution)/shard_map/psum | solution.py:78
  975.3 158.5 %reduce-scatter.29.cloned.1.call-start = ((), (), s32[]{:S(2)}) async-start(), calls=%async_computation.21 | async-start | bytes 516096 | tf_op jit(solution)/shard_map/reduce_scatter | solution.py:63
  1086.5 7.1 collective-permute-start.7
  1096.1 169.2 %all-reduce.22.cloned.1.call-start = ((), (), s32[]{:S(2)}) async-start(), calls=%async_computation.22 | async-start | bytes 2097152 | tf_op jit(solution)/shard_map/psum | solution.py:43
  (51 other events, 1047.8 us)
Sparse Core Ops, SparseCore 0:
  29.1 36.0 reduce-scatter.10
  85.5 91.3 all-reduce.17
  183.9 35.8 reduce-scatter.20
  222.9 35.4 reduce-scatter.12
  293.9 93.1 all-reduce.27
  415.6 34.8 reduce-scatter.14
  453.8 35.4 reduce-scatter.22
  524.9 93.3 all-reduce.25
  648.0 34.8 reduce-scatter.16
  686.0 35.4 reduce-scatter.24
  757.6 93.2 all-reduce.23
  880.2 34.8 reduce-scatter.18
  918.2 35.5 reduce-scatter.26
  975.4 91.5 all-reduce.19
  1096.2 37.5 reduce-scatter.28
  1171.9 93.3 all-reduce.21
where the time goes:
time: 1290 us
  waiting for transfers between devices  869 us (67%)
  blocking collectives  278 us (22%)
  matrix products  72.4 us (6%)
  other arithmetic  35.3 us (3%)
  starting transfers between devices  18.5 us (1%)
  between operations  14.4 us (1%)
    psum x5, waiting for transfers between devices, section_forward(): lax.psum(jnp.dot(hidden, weight_out, preferred_element_type=jnp.float32),...  452 us
    reduce_scatter x5, waiting for transfers between devices, section_backward(): lax.psum_scatter(lax.dot_general(grad_out, weight_out, contract_last, pre...  160 us
    reduce_scatter x5, waiting for transfers between devices, section_forward(): lax.psum_scatter(jnp.dot(normed_bf, weight_in, preferred_element_type=jnp...  130 us
    psum x1, waiting for transfers between devices, section_backward(): lax.psum(lax.dot_general(grad_pre, weight_in, contract_last, preferred_el...  88 us
    psum x5, blocking collectives, section_forward(): lax.psum((jnp.sum(values, 1), jnp.sum(values * values, 1)), 'dp')  84.6 us
    all_gather x5, blocking collectives, section_backward(): lax.all_gather((grad_share * gelu_slope(pre_share)).astype(jnp.bfloat16),...  82.9 us
    all_gather x5, blocking collectives, section_forward(): lax.all_gather(gelu_value(pre_share).astype(jnp.bfloat16), 'dp', axis=0,...  78.4 us
    ppermute x8, waiting for transfers between devices, passed_along(): return lax.ppermute(block, axis, route)  37.9 us
  transfers between devices with their start and end apart: 24, of which 24 were waited for; matrix products, arithmetic and copies ran while one was open for 4% of the time, Pallas kernels for 0%

commit v1 on v0

v1 whole, which is shorter than its diff:
```python
import jax
import jax.numpy as jnp
from jax import lax
from jax.sharding import PartitionSpec as P

root_two_pi = 0.7978845608
LANES = 128
EVERYWHERE = ("section", "dp", "tensor")
f32 = jnp.float32
bf16 = jnp.bfloat16


def gelu_value(pre_act):
    inner = jnp.tanh(root_two_pi * (pre_act + 0.044715 * pre_act**3))
    return 0.5 * pre_act * (1.0 + inner)


def gelu_slope(pre_act):
    inner = jnp.tanh(root_two_pi * (pre_act + 0.044715 * pre_act**3))
    return 0.5 * (1.0 + inner) + 0.5 * pre_act * (1.0 - inner * inner) * root_two_pi * (
        1.0 + 3.0 * 0.044715 * pre_act * pre_act
    )


def matmul(a, b):
    return jnp.dot(a, b, preferred_element_type=f32)


def matmul_t(a, b):
    return lax.dot_general(a, b, (((1,), (1,)), ((), ())), preferred_element_type=f32)


def matmul_ta(a, b):
    return lax.dot_general(a, b, (((0,), (0,)), ((), ())), preferred_element_type=f32)


def three_parts(value):
    high = lax.reduce_precision(value, 8, 7)
    rest = value - high
    middle = lax.reduce_precision(rest, 8, 7)
    return high, middle, rest - middle


def pack_side(columns):
    lane = lax.broadcasted_iota(jnp.int32, (1, LANES), 1)
    block = jnp.zeros((columns[0].shape[0], LANES), f32)
    for number, column in enumerate(columns):
        for part_no, part in enumerate(three_parts(column)):
            block = jnp.where(lane == 3 * number + part_no, part, block)
    return block.astype(bf16)


def side_value(block, number):
    lane = lax.broadcasted_iota(jnp.int32, block.shape, block.ndim - 1)
    kept = jnp.where(lane // 3 == number, block.astype(f32), 0.0)
    return jnp.sum(kept, axis=-1, keepdims=True)


def z_route(step, sections, dp_size, tensor_size):
    route = []
    for section in sections:
        for place in range(dp_size):
            other = ((place // 2) ^ step) * 2 + place % 2
            for column in range(tensor_size):
                route.append(
                    (
                        (section * dp_size + place) * tensor_size + column,
                        (section * dp_size + other) * tensor_size + column,
                    )
                )
    return route


def body(tokens, w_in, w_out, cotangent):
    dp_size = lax.axis_size("dp")
    tensor_size = lax.axis_size("tensor")
    z_size = dp_size // 2
    micro, rows_each, own_width = tokens.shape
    rows = micro * rows_each
    half = rows // 2
    z_rows = half // z_size
    t_rows = half // tensor_size
    width = own_width * dp_size
    pair_width = 2 * own_width
    units = w_in.shape[2]
    first_section = lax.axis_index("section") == 0
    place = lax.axis_index("dp")
    z_place, core = place // 2, place % 2
    t_place = lax.axis_index("tensor")

    def pick(early, later):
        return jnp.where(first_section, early, later)

    def core_swap(block):
        return lax.ppermute(block, "dp", [(i, i ^ 1) for i in range(dp_size)])

    def section_hop(block, source):
        return lax.ppermute(block, "section", [(source, 1 - source)])

    def reorder(block):
        parts = block.reshape(2, 2, 2, z_rows, block.shape[1])
        for axis, bit in ((0, core), (1, z_place // 2), (2, z_place % 2)):
            low = lax.index_in_dim(parts, 0, axis)
            high = lax.index_in_dim(parts, 1, axis)
            parts = jnp.concatenate(
                [jnp.where(bit == 1, high, low), jnp.where(bit == 1, low, high)], axis
            )
        return parts.reshape(block.shape)

    def z_blocks(blocks, sections):
        return [blocks[0]] + [
            lax.ppermute(blocks[step], EVERYWHERE, z_route(step, sections, dp_size, tensor_size))
            for step in range(1, z_size)
        ]

    def z_scatter(block, sections):
        return z_blocks([block[k * z_rows : (k + 1) * z_rows] for k in range(z_size)], sections)

    def z_gather(block, sections):
        return jnp.concatenate(z_blocks([block] * z_size, sections), 0)

    def t_scatter(block):
        blocks = block.reshape(tensor_size, t_rows, block.shape[1])
        parts = lax.all_to_all(blocks, "tensor", 0, 0)
        return jnp.sum(parts.astype(f32), 0)

    def t_gather(block):
        copies = jnp.broadcast_to(block[None], (tensor_size,) + block.shape)
        return lax.all_to_all(copies, "tensor", 0, 0)

    def t_slab(block):
        return lax.dynamic_slice_in_dim(block, t_place * t_rows, t_rows, 0)

    def own_columns(block):
        return jnp.concatenate([block[:, :own_width], core_swap(block[:, own_width:])], 0)

    def forward_partial(block):
        values = block.astype(f32)
        total = jnp.sum(values, 1, keepdims=True)
        squares = jnp.sum(values * values, 1, keepdims=True)
        product = matmul(block, w_in_pair) - (total / pair_width) * column_sum
        return jnp.concatenate([product.astype(bf16), pack_side([total, squares])], 1)

    def finish_pre(blocks, sums):
        sides = [block[:, units:] for block in blocks]
        totals = [side_value(side, 0) for side in sides]
        squares = sum(side_value(side, 1) for side in sides)
        mean = sum(totals) / width
        inv_scale = lax.rsqrt(squares / width - mean * mean + 1e-05)
        product = sum(block[:, :units].astype(f32) for block in blocks)
        for total, its_sum in zip(totals, sums):
            product = product + (total / pair_width - mean) * its_sum
        return product * inv_scale, mean, inv_scale

    def backward_sums(grad_pre, pre):
        values = grad_pre.astype(f32)
        first = jnp.sum(values * sum(sums), 1, keepdims=True)
        second = jnp.sum(values * pre, 1, keepdims=True)
        return first, second

    def input_gradient(grad_slab, total, input_slab, side):
        first = side_value(total[:, pair_width:], 2) / width
        second = side_value(total[:, pair_width:], 3) / width
        mean, inv_scale = side_value(t_slab(side), 0), side_value(t_slab(side), 1)
        normed = (input_slab.astype(f32) - mean) * inv_scale
        return (
            grad_slab.astype(f32) + inv_scale * (total[:, :pair_width] - first - normed * second)
        ).astype(bf16)

    with jax.named_scope("tick0"):
        w_in_own, w_out_own = w_in[0], w_out[0]
        w_in_pair = jnp.concatenate([w_in_own, core_swap(w_in_own)], 0)
        w_out_pair = jnp.concatenate([w_out_own, core_swap(w_out_own)], 1)
        in_own = reorder(pick(tokens, cotangent).reshape(rows, own_width))
        in_half = jnp.concatenate([in_own[:half], core_swap(in_own[half:])], 1)
        in_slab = t_slab(in_half)
        column_sum = jnp.sum(w_in_pair.astype(f32), 0, keepdims=True)
        sum_rows = jnp.concatenate(
            list(three_parts(column_sum)) + [jnp.zeros((13, units), f32)], 0
        ).astype(bf16)
        sum_rows = jnp.concatenate([sum_rows, jnp.zeros((16, LANES), bf16)], 1)
        grad_partial = matmul_t(in_half, w_out_pair).astype(bf16)
        grad_partial = jnp.concatenate([grad_partial, jnp.zeros((half, LANES), bf16)], 1)
        partial = pick(forward_partial(in_half), grad_partial)
        blocks = z_blocks(
            [
                jnp.concatenate([partial[k * z_rows : (k + 1) * z_rows], sum_rows], 0)
                for k in range(z_size)
            ],
            (0, 1),
        )
        sums = [
            jnp.sum(block[z_rows : z_rows + 3, :units].astype(f32), 0, keepdims=True)
            for block in blocks
        ]
        blocks = [block[:z_rows] for block in blocks]
        pre_early, mean_early, scale_early = finish_pre(blocks, sums)
        grad_hidden_later = sum(block[:, :units].astype(f32) for block in blocks)
        hidden = gelu_value(pre_early).astype(bf16)
        hidden_early = z_gather(
            jnp.concatenate([hidden, pack_side([mean_early, scale_early])], 1), (0,)
        )
        branch = t_scatter(matmul(hidden_early[:, :units], w_out_pair).astype(bf16))
        middle_slab = (in_slab.astype(f32) + branch).astype(bf16)
        middle_slab = pick(middle_slab, section_hop(middle_slab, 0))
        middle = t_gather(middle_slab).reshape(half, pair_width)

    with jax.named_scope("tick1"):
        blocks = z_scatter(forward_partial(middle), (1,))
        pre_later, mean_later, scale_later = finish_pre(blocks, sums)
        hidden_share = gelu_value(pre_later).astype(bf16)
        grad_pre = (grad_hidden_later * gelu_slope(pre_later)).astype(bf16)
        side = pack_side([mean_later, scale_later, *backward_sums(grad_pre, pre_later)])
        grad_pre_later = z_gather(jnp.concatenate([grad_pre, side], 1), (1,))
        partial = matmul_t(grad_pre_later[:, :units], w_in_pair).astype(bf16)
        total = t_scatter(jnp.concatenate([partial, grad_pre_later[:, units:]], 1))
        turn_slab = input_gradient(in_slab, total, middle_slab, grad_pre_later[:, units:])
        turn_slab = pick(section_hop(turn_slab, 1), turn_slab)
        turn = t_gather(turn_slab).reshape(half, pair_width)

    with jax.named_scope("tick2"):
        blocks = z_scatter(matmul_t(turn, w_out_pair).astype(bf16), (0,))
        grad_hidden = sum(block.astype(f32) for block in blocks)
        grad_pre = (grad_hidden * gelu_slope(pre_early)).astype(bf16)
        side = pack_side([mean_early, scale_early, *backward_sums(grad_pre, pre_early)])
        share = jnp.concatenate([pick(grad_pre, hidden_share), side], 1)
        last = z_gather(share, (0, 1))
        partial = pick(
            matmul_t(last[:, :units], w_in_pair), matmul(last[:, :units], w_out_pair)
        ).astype(bf16)
        total = t_scatter(jnp.concatenate([partial, last[:, units:]], 1))
        final_slab = pick(
            input_gradient(turn_slab, total, in_slab, last[:, units:]),
            (middle_slab.astype(f32) + total[:, :pair_width]).astype(bf16),
        )
        final = t_gather(own_columns(final_slab).reshape(2, t_rows, own_width))
        final = jnp.swapaxes(final, 0, 1).reshape(rows, own_width)

    with jax.named_scope("weights"):
        middle_own = own_columns(middle)
        turn_own = own_columns(turn)
        grad_pre_half = pick(last, grad_pre_later)
        hidden_half = pick(hidden_early, last)
        grad_pre_all = jnp.concatenate([grad_pre_half, core_swap(grad_pre_half)], 0)
        hidden_all = jnp.concatenate([hidden_half, core_swap(hidden_half)], 0)
        side = grad_pre_all[:, units:]
        section_input = pick(in_own, middle_own).astype(f32)
        normed = ((section_input - side_value(side, 0)) * side_value(side, 1)).astype(bf16)
        grad_out = pick(turn_own, in_own)
        grad_w_in = matmul_ta(normed, grad_pre_all[:, :units]).astype(bf16)
        grad_w_out = matmul_ta(hidden_all[:, :units], grad_out).astype(bf16)

    shape = (1,) + tokens.shape
    return (
        reorder(pick(middle_own, final)).reshape(shape),
        reorder(pick(final, turn_own)).reshape(shape),
        grad_w_in[None],
        grad_w_out[None],
    )


def solution(mesh):
    in_specs = (
        P(None, None, "dp"),
        P("section", "dp", "tensor"),
        P("section", "tensor", "dp"),
        P(None, None, "dp"),
    )
    out_specs = (
        P("section", None, None, "dp"),
        P("section", None, None, "dp"),
        P("section", "dp", "tensor"),
        P("section", "tensor", "dp"),
    )
    return jax.shard_map(body, mesh=mesh, in_specs=in_specs, out_specs=out_specs, check_vma=False)
```

time: 1290 us -> 293 us (0.23)
  waiting for transfers between devices: 869 us -> 108 us
  blocking collectives: 278 us -> 60.9 us
  starting transfers between devices: 18.5 us -> 72.9 us
  matrix products: 72.4 us -> 19.8 us
  other arithmetic: 35.3 us -> 19.4 us
    psum x6 -> x0, waiting for transfers between devices: 540 us -> none  [the longest x5 452 us: section_forward(): lax.psum(jnp.dot(hidden, weight_out, preferred_element_type=jnp.float32),...]
    reduce_scatter x10 -> x0, waiting for transfers between devices: 291 us -> none  [the longest x5 160 us: section_backward(): lax.psum_scatter(lax.dot_general(grad_out, weight_out, contract_last, pre...]
    all_gather x10 -> x0, blocking collectives: 161 us -> none  [the longest x5 82.9 us: section_backward(): lax.all_gather((grad_share * gelu_slope(pre_share)).astype(jnp.bfloat16),...]
    psum x7 -> x0, blocking collectives: 117 us -> none  [the longest x5 84.6 us: section_forward(): lax.psum((jnp.sum(values, 1), jnp.sum(values * values, 1)), 'dp')]
    all_to_all x0 -> x3, blocking collectives: none -> 60.9 us  [the longest x2 45.7 us: t_scatter(): parts = lax.all_to_all(blocks, 'tensor', 0, 0)]
    dot_general x30 -> x10, matrix products: 72.4 us -> 19.8 us  [the longest x4 8.19 us: matmul(): return jnp.dot(a, b, preferred_element_type=f32)]
    ppermute x8 -> x28, starting transfers between devices: 17.8 us -> 56.1 us  [the longest x18 45.3 us: z_blocks(): lax.ppermute(blocks[step], EVERYWHERE, z_route(step, sections, dp_size, t...]
    all_to_all x0 -> x3, waiting for transfers between devices: none -> 37.6 us  [the longest x2 23 us: t_gather(): return lax.all_to_all(copies, 'tensor', 0, 0)]
  transfers between devices with their start and end apart: 24 -> 31, of which waited for: 24 -> 16; matrix products, arithmetic and copies ran while one was open for 4% -> 5% of each run, Pallas kernels for 0% -> 0%
where the time goes in v1:
time: 293 us; the launch traced here: 292 us
  waiting for transfers between devices  108 us (37%)
  starting transfers between devices  72.9 us (25%)
  blocking collectives  60.9 us (21%)
  matrix products  19.8 us (7%)
  other arithmetic  19.4 us (7%)
  local copies, waits for them, and re-layouts  8.81 us (3%)
    all_to_all x2, blocking collectives, t_scatter(): parts = lax.all_to_all(blocks, 'tensor', 0, 0)  45.7 us
    ppermute x18, starting transfers between devices, z_blocks(): lax.ppermute(blocks[step], EVERYWHERE, z_route(step, sections, dp_size, t...  45.3 us
    ppermute x2, waiting for transfers between devices, section_hop(): return lax.ppermute(block, 'section', [(source, 1 - source)])  35.2 us
    ppermute x18, waiting for transfers between devices, z_blocks(): lax.ppermute(blocks[step], EVERYWHERE, z_route(step, sections, dp_size, t...  31.9 us
    all_to_all x2, waiting for transfers between devices, t_gather(): return lax.all_to_all(copies, 'tensor', 0, 0)  23 us
    all_to_all x1, blocking collectives, t_gather(): return lax.all_to_all(copies, 'tensor', 0, 0)  15.2 us
    all_to_all x1, waiting for transfers between devices, t_scatter(): parts = lax.all_to_all(blocks, 'tensor', 0, 0)  14.6 us
    all_to_all x2, starting transfers between devices, t_gather(): return lax.all_to_all(copies, 'tensor', 0, 0)  9.61 us
  transfers between devices with their start and end apart: 31, of which 16 were waited for; matrix products, arithmetic and copies ran while one was open for 5% of the time, Pallas kernels for 0%

profile of v1, /device:TPU:1, one launch (start us, length us, event | category | flops | bytes accessed | tf_op | source)
XLA Modules:
  0.0 292.0 jit_solution(6316455731350525830)
XLA Ops:
  0.6 3.3 %collective-permute-start.1 = (bf16[1024,896]{1,0:T(8,128)(2,1)}, bf16[1024,896]{1,0:T(8,128)(2,1)S(1)}, u32[]{:S(2)}, u32[]{:S(2)}) collective-permute-start(bf16[1024,896]{1,0:T(8,128)(2,1)} %bitcast.49), channel_id=1, source_target_pairs={{0,16},{16,0},{32,48},{48,32},{64,80},{80,64},{96,112},{112,96},{1... | collective-permute-start | bytes 5505032 | tf_op jit(solution)/shard_map/tick0/ppermute | solution.py:95
  15.0 5.1 %collective-permute-start.4 = (bf16[80,1024]{1,0:T(8,128)(2,1)S(1)}, bf16[80,1024]{1,0:T(8,128)(2,1)S(1)}, u32[]{:S(2)}, u32[]{:S(2)}) collective-permute-start(bf16[80,1024]{1,0:T(8,128)(2,1)S(1)} %get-tuple-element.110), channel_id=1, source_target_pairs={{0,64},{1,65},{2,66},{3,67},{4,68},{5,69},{6,70},{7,71},{8,72},{9,... | collective-permute-start | bytes 491528 | tf_op jit(solution)/shard_map/tick0/ppermute | solution.py:112
  20.2 7.6 %collective-permute-done.3 = bf16[80,1024]{1,0:T(8,128)(2,1)S(1)} collective-permute-done((bf16[80,1024]{1,0:T(8,128)(2,1)S(1)}, bf16[80,1024]{1,0:T(8,128)(2,1)S(1)}, u32[]{:S(2)}, u32[]{:S(2)}) %collective-permute-start.3) | collective-permute-done | bytes 163872 | tf_op jit(solution)/shard_map/tick0/ppermute | solution.py:112
  27.8 4.5 %collective-permute-done.4 = bf16[80,1024]{1,0:T(8,128)(2,1)S(1)} collective-permute-done((bf16[80,1024]{1,0:T(8,128)(2,1)S(1)}, bf16[80,1024]{1,0:T(8,128)(2,1)S(1)}, u32[]{:S(2)}, u32[]{:S(2)}) %collective-permute-start.4) | collective-permute-done | bytes 163872 | tf_op jit(solution)/shard_map/tick0/ppermute | solution.py:112
  33.5 6.4 %collective-permute-start.6 = (bf16[64,1024]{1,0:T(8,128)(2,1)S(1)}, bf16[64,1024]{1,0:T(8,128)(2,1)S(1)}, u32[]{:S(2)}, u32[]{:S(2)}) collective-permute-start(bf16[64,1024]{1,0:T(8,128)(2,1)S(1)} %pad_maximum_fusion.27), channel_id=1, source_target_pairs={{0,32},{1,33},{2,34},{3,35},{4,36},{5,37},{6,38},{7,39},{8,40},{9,... | collective-permute-start | bytes 393224 | tf_op jit(solution)/shard_map/tick0/ppermute | solution.py:112
  39.8 3.9 %collective-permute-start.7 = (bf16[64,1024]{1,0:T(8,128)(2,1)S(1)}, bf16[64,1024]{1,0:T(8,128)(2,1)S(1)}, u32[]{:S(2)}, u32[]{:S(2)}) collective-permute-start(bf16[64,1024]{1,0:T(8,128)(2,1)S(1)} %pad_maximum_fusion.27), channel_id=1, source_target_pairs={{0,64},{1,65},{2,66},{3,67},{4,68},{5,69},{6,70},{7,71},{8,72},{9,... | collective-permute-start | bytes 393224 | tf_op jit(solution)/shard_map/tick0/ppermute | solution.py:112
  49.6 3.6 %collective-permute-done.8 = bf16[64,1024]{1,0:T(8,128)(2,1)S(1)} collective-permute-done((bf16[64,1024]{1,0:T(8,128)(2,1)S(1)}, bf16[64,1024]{1,0:T(8,128)(2,1)S(1)}, u32[]{:S(2)}, u32[]{:S(2)}) %collective-permute-start.8) | collective-permute-done | bytes 131104 | tf_op jit(solution)/shard_map/tick0/ppermute | solution.py:112
  55.6 7.2 %all-to-all-start = ((bf16[16,16,2048]{2,1,0:T(8,128)(2,1)}), bf16[16,16,2048]{2,1,0:T(8,128)(2,1)S(1)}, u32[]{:S(2)}, u32[]{:S(2)}) async-start(bf16[16,16,2048]{2,1,0:T(8,128)(2,1)} %bitcast.57), calls=%async_computation | async-start | bytes 2097152 | tf_op jit(solution)/shard_map/tick0/all_to_all | solution.py:124
  62.8 14.6 %all-to-all-done = bf16[16,16,2048]{2,1,0:T(8,128)(2,1)S(1)} async-done(((bf16[16,16,2048]{2,1,0:T(8,128)(2,1)}), bf16[16,16,2048]{2,1,0:T(8,128)(2,1)S(1)}, u32[]{:S(2)}, u32[]{:S(2)}) %all-to-all-start) | async-done | bytes 1048608 | tf_op jit(solution)/shard_map/tick0/all_to_all | solution.py:124
  82.6 5.1 %all-to-all-start.1 = ((bf16[16,16,2048]{2,1,0:T(8,128)(2,1)}), bf16[16,16,2048]{2,1,0:T(8,128)(2,1)S(1)}, u32[]{:S(2)}, u32[]{:S(2)}) async-start(bf16[16,16,2048]{2,1,0:T(8,128)(2,1)} %broadcast_in_dim.538), calls=%async_computation.1 | async-start | bytes 2097152 | tf_op jit(solution)/shard_map/tick0/all_to_all | solution.py:129
  91.0 11.3 %all-to-all-done.1 = bf16[16,16,2048]{2,1,0:T(8,128)(2,1)S(1)} async-done(((bf16[16,16,2048]{2,1,0:T(8,128)(2,1)}), bf16[16,16,2048]{2,1,0:T(8,128)(2,1)S(1)}, u32[]{:S(2)}, u32[]{:S(2)}) %all-to-all-start.1) | async-done | bytes 1048608 | tf_op jit(solution)/shard_map/tick0/all_to_all | solution.py:129
  103.3 3.4 %fusion.4 = bf16[256,896]{1,0:T(8,128)(2,1)S(1)} fusion(bf16[256,2048]{1,0:T(8,128)(2,1)S(1)} %bitcast.33, f32[256]{0:T(256)S(1)} %broadcast_multiply_fusion, f32[896]{0:T(1024)S(1)} %convert_reduce_fusion, bf16[1024,896]{1,0:T(8,128)(2,1)} %copy-done.9, bf16[1024,896]{1,0:T(8,128)(2,1)} %bitcast.50), kind=kOutput, calls=%fused_computation.27 | convolution fusion | flops 947552256 | bytes 5181952 | tf_op jit(solution)/shard_map/tick1/dot_general | solution.py:26
  114.7 20.4 %all_to_all.30 = bf16[16,16,2176]{2,1,0:T(8,128)(2,1)S(1)} all-to-all(bf16[16,16,2176]{2,1,0:T(8,128)(2,1)S(1)} %bitcast.39), channel_id=1, replica_groups=mesh['section'=2,'dp'=8,'tensor'=16] {'tensor'}, dimensions={0} | all-to-all | bytes 2228224 | tf_op jit(solution)/shard_map/tick1/all_to_all | solution.py:124
  137.2 33.9 %collective-permute-done.17 = bf16[16,2048]{1,0:T(8,128)(2,1)S(1)} collective-permute-done((bf16[16,2048]{1,0:T(8,128)(2,1)S(1)}, bf16[16,2048]{1,0:T(8,128)(2,1)S(1)}, u32[]{:S(2)}, u32[]{:S(2)}) %collective-permute-start.17) | collective-permute-done | bytes 65568 | tf_op jit(solution)/shard_map/tick1/ppermute | solution.py:98
  171.1 15.2 %all_to_all.31 = bf16[16,16,2048]{2,1,0:T(8,128)(2,1)S(1)} all-to-all(bf16[16,16,2048]{2,1,0:T(8,128)(2,1)S(1)} %broadcast_in_dim.564), channel_id=1, replica_groups=mesh['section'=2,'dp'=8,'tensor'=16] {'tensor'}, dimensions={0} | all-to-all | bytes 2097152 | tf_op jit(solution)/shard_map/tick1/all_to_all | solution.py:129
  187.9 4.2 %collective-permute-start.18 = (bf16[64,896]{1,0:T(8,128)(2,1)S(1)}, bf16[64,896]{1,0:T(8,128)(2,1)S(1)}, u32[]{:S(2)}, u32[]{:S(2)}) collective-permute-start(bf16[64,896]{1,0:T(8,128)(2,1)S(1)} %get-tuple-element.105), channel_id=1, source_target_pairs={{0,32},{1,33},{2,34},{3,35},{4,36},{5,37},{6,38},{7,39},{8,40},{9,... | collective-permute-start | bytes 344072 | tf_op jit(solution)/shard_map/tick2/ppermute | solution.py:112
  192.1 9.2 %collective-permute-start.19 = (bf16[64,896]{1,0:T(8,128)(2,1)S(1)}, bf16[64,896]{1,0:T(8,128)(2,1)S(1)}, u32[]{:S(2)}, u32[]{:S(2)}) collective-permute-start(bf16[64,896]{1,0:T(8,128)(2,1)S(1)} %get-tuple-element.107), channel_id=1, source_target_pairs={{0,64},{1,65},{2,66},{3,67},{4,68},{5,69},{6,70},{7,71},{8,72},{9,... | collective-permute-start | bytes 344072 | tf_op jit(solution)/shard_map/tick2/ppermute | solution.py:112
  205.0 6.4 %collective-permute-done.20 = bf16[64,896]{1,0:T(8,128)(2,1)S(1)} collective-permute-done((bf16[64,896]{1,0:T(8,128)(2,1)S(1)}, bf16[64,896]{1,0:T(8,128)(2,1)S(1)}, u32[]{:S(2)}, u32[]{:S(2)}) %collective-permute-start.20) | collective-permute-done | bytes 114720 | tf_op jit(solution)/shard_map/tick2/ppermute | solution.py:112
  212.2 5.1 %collective-permute-start.22 = (bf16[64,1024]{1,0:T(8,128)(2,1)S(1)}, bf16[64,1024]{1,0:T(8,128)(2,1)S(1)}, u32[]{:S(2)}, u32[]{:S(2)}) collective-permute-start(bf16[64,1024]{1,0:T(8,128)(2,1)S(1)} %pad_maximum_fusion.29), channel_id=1, source_target_pairs={{0,64},{1,65},{2,66},{3,67},{4,68},{5,69},{6,70},{7,71},{8,72},{9,... | collective-permute-start | bytes 393224 | tf_op jit(solution)/shard_map/tick2/ppermute | solution.py:112
  217.8 5.3 %collective-permute-done.22 = bf16[64,1024]{1,0:T(8,128)(2,1)S(1)} collective-permute-done((bf16[64,1024]{1,0:T(8,128)(2,1)S(1)}, bf16[64,1024]{1,0:T(8,128)(2,1)S(1)}, u32[]{:S(2)}, u32[]{:S(2)}) %collective-permute-start.22) | collective-permute-done | bytes 131104 | tf_op jit(solution)/shard_map/tick2/ppermute | solution.py:112
  227.1 25.3 %all_to_all.32 = bf16[16,16,2176]{2,1,0:T(8,128)(2,1)S(1)} all-to-all(bf16[16,16,2176]{2,1,0:T(8,128)(2,1)S(1)} %bitcast.40), channel_id=1, replica_groups=mesh['section'=2,'dp'=8,'tensor'=16] {'tensor'}, dimensions={0} | all-to-all | bytes 2228224 | tf_op jit(solution)/shard_map/tick2/all_to_all | solution.py:124
  257.9 4.5 %all-to-all-start.5 = ((bf16[16,2,16,1024]{3,2,1,0:T(8,128)(2,1)}), bf16[16,2,16,1024]{3,2,1,0:T(8,128)(2,1)}, u32[]{:S(2)}, u32[]{:S(2)}) async-start(bf16[16,2,16,1024]{3,2,1,0:T(8,128)(2,1)} %broadcast_in_dim.572), calls=%async_computation.5 | async-start | bytes 2097152 | tf_op jit(solution)/shard_map/tick2/all_to_all | solution.py:129
  267.4 11.7 %all-to-all-done.5 = bf16[16,2,16,1024]{3,2,1,0:T(8,128)(2,1)} async-done(((bf16[16,2,16,1024]{3,2,1,0:T(8,128)(2,1)}), bf16[16,2,16,1024]{3,2,1,0:T(8,128)(2,1)}, u32[]{:S(2)}, u32[]{:S(2)}) %all-to-all-start.5) | async-done | bytes 1048608 | tf_op jit(solution)/shard_map/tick2/all_to_all | solution.py:129
  285.7 3.6 %convert_bitcast_fusion = bf16[1,896,1024]{2,1,0:T(8,128)(2,1)} fusion(bf16[512,1024]{1,0:T(8,128)(2,1)S(1)} %get-tuple-element.69, bf16[256,1024]{1,0:T(8,128)(2,1)} %collective-permute-done.27, bf16[256,1024]{1,0:T(8,128)(2,1)} %get-tuple-element.97), kind=kOutput, calls=%fused_computation.17 | convolution fusion | flops 942276608 | bytes 3932160 | tf_op jit(solution)/shard_map/weights/dot_general | solution.py:34
  (350 shorter events, 68.8 us)
Async XLA Ops:
  0.6 8.2 %collective-permute-start.1 = (bf16[1024,896]{1,0:T(8,128)(2,1)}, bf16[1024,896]{1,0:T(8,128)(2,1)S(1)}, u32[]{:S(2)}, u32[]{:S(2)}) collective-permute-start(bf16[1024,896]{1,0:T(8,128)(2,1)} %bitcast.49), channel_id=1, source_target_pairs={{0,16},{16,0},{32,48},{48,32},{64,80},{80,64},{96,112},{112,96},{1... | collective-permute-start | bytes 5505032 | tf_op jit(solution)/shard_map/tick0/ppermute | solution.py:95
  5.7 2.4 collective-permute-start
  7.0 3.8 %collective-permute-start.2 = (bf16[896,1024]{1,0:T(8,128)(2,1)S(1)}, bf16[896,1024]{1,0:T(8,128)(2,1)S(1)}, u32[]{:S(2)}, u32[]{:S(2)}) collective-permute-start(bf16[896,1024]{1,0:T(8,128)(2,1)S(1)} %bitcast.60), channel_id=1, source_target_pairs={{0,16},{16,0},{32,48},{48,32},{64,80},{80,64},{96,112},{112,96},{1... | collective-permute-start | bytes 5505032 | tf_op jit(solution)/shard_map/tick0/ppermute | solution.py:95
  13.6 14.1 %collective-permute-start.3 = (bf16[80,1024]{1,0:T(8,128)(2,1)S(1)}, bf16[80,1024]{1,0:T(8,128)(2,1)S(1)}, u32[]{:S(2)}, u32[]{:S(2)}) collective-permute-start(bf16[80,1024]{1,0:T(8,128)(2,1)S(1)} %get-tuple-element.111), channel_id=1, source_target_pairs={{0,32},{1,33},{2,34},{3,35},{4,36},{5,37},{6,38},{7,39},{8,40},{9,... | collective-permute-start | bytes 491528 | tf_op jit(solution)/shard_map/tick0/ppermute | solution.py:112
  15.0 17.3 %collective-permute-start.4 = (bf16[80,1024]{1,0:T(8,128)(2,1)S(1)}, bf16[80,1024]{1,0:T(8,128)(2,1)S(1)}, u32[]{:S(2)}, u32[]{:S(2)}) collective-permute-start(bf16[80,1024]{1,0:T(8,128)(2,1)S(1)} %get-tuple-element.110), channel_id=1, source_target_pairs={{0,64},{1,65},{2,66},{3,67},{4,68},{5,69},{6,70},{7,71},{8,72},{9,... | collective-permute-start | bytes 491528 | tf_op jit(solution)/shard_map/tick0/ppermute | solution.py:112
  20.1 12.2 %collective-permute-start.5 = (bf16[80,1024]{1,0:T(8,128)(2,1)S(1)}, bf16[80,1024]{1,0:T(8,128)(2,1)S(1)}, u32[]{:S(2)}, u32[]{:S(2)}) collective-permute-start(bf16[80,1024]{1,0:T(8,128)(2,1)S(1)} %get-tuple-element.112), channel_id=1, source_target_pairs={{0,96},{1,97},{2,98},{3,99},{4,100},{5,101},{6,102},{7,103},{8,104... | collective-permute-start | bytes 491528 | tf_op jit(solution)/shard_map/tick0/ppermute | solution.py:112
  33.5 13.5 %collective-permute-start.6 = (bf16[64,1024]{1,0:T(8,128)(2,1)S(1)}, bf16[64,1024]{1,0:T(8,128)(2,1)S(1)}, u32[]{:S(2)}, u32[]{:S(2)}) collective-permute-start(bf16[64,1024]{1,0:T(8,128)(2,1)S(1)} %pad_maximum_fusion.27), channel_id=1, source_target_pairs={{0,32},{1,33},{2,34},{3,35},{4,36},{5,37},{6,38},{7,39},{8,40},{9,... | collective-permute-start | bytes 393224 | tf_op jit(solution)/shard_map/tick0/ppermute | solution.py:112
  39.8 9.7 %collective-permute-start.7 = (bf16[64,1024]{1,0:T(8,128)(2,1)S(1)}, bf16[64,1024]{1,0:T(8,128)(2,1)S(1)}, u32[]{:S(2)}, u32[]{:S(2)}) collective-permute-start(bf16[64,1024]{1,0:T(8,128)(2,1)S(1)} %pad_maximum_fusion.27), channel_id=1, source_target_pairs={{0,64},{1,65},{2,66},{3,67},{4,68},{5,69},{6,70},{7,71},{8,72},{9,... | collective-permute-start | bytes 393224 | tf_op jit(solution)/shard_map/tick0/ppermute | solution.py:112
  43.7 9.5 %collective-permute-start.8 = (bf16[64,1024]{1,0:T(8,128)(2,1)S(1)}, bf16[64,1024]{1,0:T(8,128)(2,1)S(1)}, u32[]{:S(2)}, u32[]{:S(2)}) collective-permute-start(bf16[64,1024]{1,0:T(8,128)(2,1)S(1)} %pad_maximum_fusion.27), channel_id=1, source_target_pairs={{0,96},{1,97},{2,98},{3,99},{4,100},{5,101},{6,102},{7,103},{8,104... | collective-permute-start | bytes 393224 | tf_op jit(solution)/shard_map/tick0/ppermute | solution.py:112
  55.6 21.8 %all-to-all-start = ((bf16[16,16,2048]{2,1,0:T(8,128)(2,1)}), bf16[16,16,2048]{2,1,0:T(8,128)(2,1)S(1)}, u32[]{:S(2)}, u32[]{:S(2)}) async-start(bf16[16,16,2048]{2,1,0:T(8,128)(2,1)} %bitcast.57), calls=%async_computation | async-start | bytes 2097152 | tf_op jit(solution)/shard_map/tick0/all_to_all | solution.py:124
  78.9 2.6 collective-permute-start.9
  82.6 19.6 %all-to-all-start.1 = ((bf16[16,16,2048]{2,1,0:T(8,128)(2,1)}), bf16[16,16,2048]{2,1,0:T(8,128)(2,1)S(1)}, u32[]{:S(2)}, u32[]{:S(2)}) async-start(bf16[16,16,2048]{2,1,0:T(8,128)(2,1)} %broadcast_in_dim.538), calls=%async_computation.1 | async-start | bytes 2097152 | tf_op jit(solution)/shard_map/tick0/all_to_all | solution.py:129
  135.6 35.4 %collective-permute-start.17 = (bf16[16,2048]{1,0:T(8,128)(2,1)S(1)}, bf16[16,2048]{1,0:T(8,128)(2,1)S(1)}, u32[]{:S(2)}, u32[]{:S(2)}) collective-permute-start(bf16[16,2048]{1,0:T(8,128)(2,1)S(1)} %fusion.56), channel_id=1, source_target_pairs={{128,0},{129,1},{130,2},{131,3},{132,4},{133,5},{134,6},{135,7},{1... | collective-permute-start | bytes 196616 | tf_op jit(solution)/shard_map/tick1/ppermute | solution.py:98
  187.9 15.3 %collective-permute-start.18 = (bf16[64,896]{1,0:T(8,128)(2,1)S(1)}, bf16[64,896]{1,0:T(8,128)(2,1)S(1)}, u32[]{:S(2)}, u32[]{:S(2)}) collective-permute-start(bf16[64,896]{1,0:T(8,128)(2,1)S(1)} %get-tuple-element.105), channel_id=1, source_target_pairs={{0,32},{1,33},{2,34},{3,35},{4,36},{5,37},{6,38},{7,39},{8,40},{9,... | collective-permute-start | bytes 344072 | tf_op jit(solution)/shard_map/tick2/ppermute | solution.py:112
  192.1 12.9 %collective-permute-start.19 = (bf16[64,896]{1,0:T(8,128)(2,1)S(1)}, bf16[64,896]{1,0:T(8,128)(2,1)S(1)}, u32[]{:S(2)}, u32[]{:S(2)}) collective-permute-start(bf16[64,896]{1,0:T(8,128)(2,1)S(1)} %get-tuple-element.107), channel_id=1, source_target_pairs={{0,64},{1,65},{2,66},{3,67},{4,68},{5,69},{6,70},{7,71},{8,72},{9,... | collective-permute-start | bytes 344072 | tf_op jit(solution)/shard_map/tick2/ppermute | solution.py:112
  201.3 10.1 %collective-permute-start.20 = (bf16[64,896]{1,0:T(8,128)(2,1)S(1)}, bf16[64,896]{1,0:T(8,128)(2,1)S(1)}, u32[]{:S(2)}, u32[]{:S(2)}) collective-permute-start(bf16[64,896]{1,0:T(8,128)(2,1)S(1)} %get-tuple-element.106), channel_id=1, source_target_pairs={{0,96},{1,97},{2,98},{3,99},{4,100},{5,101},{6,102},{7,103},{8,104... | collective-permute-start | bytes 344072 | tf_op jit(solution)/shard_map/tick2/ppermute | solution.py:112
  212.1 5.7 %collective-permute-start.21 = (bf16[64,1024]{1,0:T(8,128)(2,1)S(1)}, bf16[64,1024]{1,0:T(8,128)(2,1)S(1)}, u32[]{:S(2)}, u32[]{:S(2)}) collective-permute-start(bf16[64,1024]{1,0:T(8,128)(2,1)S(1)} %pad_maximum_fusion.29), channel_id=1, source_target_pairs={{0,32},{1,33},{2,34},{3,35},{4,36},{5,37},{6,38},{7,39},{8,40},{9,... | collective-permute-start | bytes 393224 | tf_op jit(solution)/shard_map/tick2/ppermute | solution.py:112
  212.2 10.9 %collective-permute-start.22 = (bf16[64,1024]{1,0:T(8,128)(2,1)S(1)}, bf16[64,1024]{1,0:T(8,128)(2,1)S(1)}, u32[]{:S(2)}, u32[]{:S(2)}) collective-permute-start(bf16[64,1024]{1,0:T(8,128)(2,1)S(1)} %pad_maximum_fusion.29), channel_id=1, source_target_pairs={{0,64},{1,65},{2,66},{3,67},{4,68},{5,69},{6,70},{7,71},{8,72},{9,... | collective-permute-start | bytes 393224 | tf_op jit(solution)/shard_map/tick2/ppermute | solution.py:112
  217.2 6.1 %collective-permute-start.23 = (bf16[64,1024]{1,0:T(8,128)(2,1)S(1)}, bf16[64,1024]{1,0:T(8,128)(2,1)S(1)}, u32[]{:S(2)}, u32[]{:S(2)}) collective-permute-start(bf16[64,1024]{1,0:T(8,128)(2,1)S(1)} %pad_maximum_fusion.29), channel_id=1, source_target_pairs={{0,96},{1,97},{2,98},{3,99},{4,100},{5,101},{6,102},{7,103},{8,104... | collective-permute-start | bytes 393224 | tf_op jit(solution)/shard_map/tick2/ppermute | solution.py:112
  252.9 3.9 %collective-permute-start.24 = (bf16[16,1024]{1,0:T(8,128)(2,1)S(1)}, bf16[16,1024]{1,0:T(8,128)(2,1)S(1)}, u32[]{:S(2)}, u32[]{:S(2)}) collective-permute-start(bf16[16,1024]{1,0:T(8,128)(2,1)S(1)} %get-tuple-element.109), channel_id=1, source_target_pairs={{0,16},{16,0},{32,48},{48,32},{64,80},{80,64},{96,112},{112,96},{1... | collective-permute-start | bytes 98312 | tf_op jit(solution)/shard_map/tick2/ppermute | solution.py:95
  257.9 21.2 %all-to-all-start.5 = ((bf16[16,2,16,1024]{3,2,1,0:T(8,128)(2,1)}), bf16[16,2,16,1024]{3,2,1,0:T(8,128)(2,1)}, u32[]{:S(2)}, u32[]{:S(2)}) async-start(bf16[16,2,16,1024]{3,2,1,0:T(8,128)(2,1)} %broadcast_in_dim.572), calls=%async_computation.5 | async-start | bytes 2097152 | tf_op jit(solution)/shard_map/tick2/all_to_all | solution.py:129
  263.5 16.9 %collective-permute-start.10 = (bf16[256,1024]{1,0:T(8,128)(2,1)}, bf16[256,1024]{1,0:T(8,128)(2,1)}, u32[]{:S(2)}, u32[]{:S(2)}) collective-permute-start(bf16[256,1024]{1,0:T(8,128)(2,1)} %get-tuple-element.88), channel_id=1, source_target_pairs={{0,16},{16,0},{32,48},{48,32},{64,80},{80,64},{96,112},{112,96},{1... | collective-permute-start | bytes 1572872 | tf_op jit(solution)/shard_map/weights/ppermute | solution.py:95
  265.7 14.8 %collective-permute-start.25 = (bf16[256,1024]{1,0:T(8,128)(2,1)}, bf16[256,1024]{1,0:T(8,128)(2,1)}, u32[]{:S(2)}, u32[]{:S(2)}) collective-permute-start(bf16[256,1024]{1,0:T(8,128)(2,1)} %get-tuple-element.80), channel_id=1, source_target_pairs={{0,16},{16,0},{32,48},{48,32},{64,80},{80,64},{96,112},{112,96},{1... | collective-permute-start | bytes 1572872 | tf_op jit(solution)/shard_map/weights/ppermute | solution.py:95
  266.0 19.7 %collective-permute-start.27 = (bf16[256,1024]{1,0:T(8,128)(2,1)}, bf16[256,1024]{1,0:T(8,128)(2,1)}, u32[]{:S(2)}, u32[]{:S(2)}) collective-permute-start(bf16[256,1024]{1,0:T(8,128)(2,1)} %get-tuple-element.97), channel_id=1, source_target_pairs={{0,16},{16,0},{32,48},{48,32},{64,80},{80,64},{96,112},{112,96},{1... | collective-permute-start | bytes 1572872 | tf_op jit(solution)/shard_map/weights/ppermute | solution.py:95
  (101 other events, 1773.0 us)

commit v2 on v1

--- a/solution.py
+++ b/solution.py
@@ -6,6 +6,7 @@
 root_two_pi = 0.7978845608
 LANES = 128
 EVERYWHERE = ("section", "dp", "tensor")
+STREAMS = 1
 f32 = jnp.float32
 bf16 = jnp.bfloat16
 
@@ -56,11 +57,11 @@
     return jnp.sum(kept, axis=-1, keepdims=True)
 
 
-def z_route(step, sections, dp_size, tensor_size):
+def z_route(dp_size, tensor_size, sections, step):
     route = []
-    for section in sections:
+    for section in (0, 1):
         for place in range(dp_size):
-            other = ((place // 2) ^ step) * 2 + place % 2
+            other = place ^ (2 * step) if section in sections else place ^ 1
             for column in range(tensor_size):
                 route.append(
                     (
@@ -76,13 +77,14 @@
     tensor_size = lax.axis_size("tensor")
     z_size = dp_size // 2
     micro, rows_each, own_width = tokens.shape
-    rows = micro * rows_each
+    rows = micro * rows_each // STREAMS
     half = rows // 2
     z_rows = half // z_size
     t_rows = half // tensor_size
     width = own_width * dp_size
     pair_width = 2 * own_width
     units = w_in.shape[2]
+    streams = range(STREAMS)
     first_section = lax.axis_index("section") == 0
     place = lax.axis_index("dp")
     z_place, core = place // 2, place % 2
@@ -97,19 +99,31 @@
     def section_hop(block, source):
         return lax.ppermute(block, "section", [(source, 1 - source)])
 
-    def reorder(block):
-        parts = block.reshape(2, 2, 2, z_rows, block.shape[1])
-        for axis, bit in ((0, core), (1, z_place // 2), (2, z_place % 2)):
-            low = lax.index_in_dim(parts, 0, axis)
-            high = lax.index_in_dim(parts, 1, axis)
-            parts = jnp.concatenate(
-                [jnp.where(bit == 1, high, low), jnp.where(bit == 1, low, high)], axis
-            )
-        return parts.reshape(block.shape)
+    def turn_axis(parts, axis, bit):
+        low = lax.index_in_dim(parts, 0, axis)
+        high = lax.index_in_dim(parts, 1, axis)
+        return jnp.concatenate(
+            [jnp.where(bit == 1, high, low), jnp.where(bit == 1, low, high)], axis
+        )
+
+    def turn_z(parts):
+        return turn_axis(turn_axis(parts, 0, z_place // 2), 1, z_place % 2)
+
+    def arrange(block):
+        parts = turn_z(block.reshape(2, 2, tensor_size // 4, 2, t_rows, block.shape[1]))
+        parts = turn_axis(parts, 3, core)
+        return jnp.concatenate([parts[:, :, :, 0], parts[:, :, :, 1]], 0).reshape(block.shape)
+
+    def arrange_back(block):
+        parts = block.reshape(2, 2, 2, tensor_size // 4, t_rows, block.shape[1])
+        parts = turn_axis(parts, 0, core)
+        return turn_z(jnp.stack([parts[0], parts[1]], 3)).reshape(block.shape)
 
     def z_blocks(blocks, sections):
         return [blocks[0]] + [
-            lax.ppermute(blocks[step], EVERYWHERE, z_route(step, sections, dp_size, tensor_size))
+            lax.ppermute(
+                blocks[step], EVERYWHERE, z_route(dp_size, tensor_size, sections, step)
+            )
             for step in range(1, z_size)
         ]
 
@@ -171,89 +185,125 @@
         w_in_own, w_out_own = w_in[0], w_out[0]
         w_in_pair = jnp.concatenate([w_in_own, core_swap(w_in_own)], 0)
         w_out_pair = jnp.concatenate([w_out_own, core_swap(w_out_own)], 1)
-        in_own = reorder(pick(tokens, cotangent).reshape(rows, own_width))
-        in_half = jnp.concatenate([in_own[:half], core_swap(in_own[half:])], 1)
-        in_slab = t_slab(in_half)
         column_sum = jnp.sum(w_in_pair.astype(f32), 0, keepdims=True)
         sum_rows = jnp.concatenate(
             list(three_parts(column_sum)) + [jnp.zeros((13, units), f32)], 0
         ).astype(bf16)
         sum_rows = jnp.concatenate([sum_rows, jnp.zeros((16, LANES), bf16)], 1)
-        grad_partial = matmul_t(in_half, w_out_pair).astype(bf16)
-        grad_partial = jnp.concatenate([grad_partial, jnp.zeros((half, LANES), bf16)], 1)
-        partial = pick(forward_partial(in_half), grad_partial)
-        blocks = z_blocks(
-            [
-                jnp.concatenate([partial[k * z_rows : (k + 1) * z_rows], sum_rows], 0)
-                for k in range(z_size)
-            ],
-            (0, 1),
-        )
+        arriving = pick(tokens, cotangent).reshape(STREAMS, rows, own_width)
+        in_own = [arrange(arriving[i]) for i in streams]
+        in_half = [jnp.concatenate([own[:half], core_swap(own[half:])], 1) for own in in_own]
+        in_slab = [t_slab(block) for block in in_half]
+        early = []
+        for i in streams:
+            grad_partial = matmul_t(in_half[i], w_out_pair).astype(bf16)
+            grad_partial = jnp.concatenate([grad_partial, jnp.zeros((half, LANES), bf16)], 1)
+            partial = pick(forward_partial(in_half[i]), grad_partial)
+            pieces = [partial[k * z_rows : (k + 1) * z_rows] for k in range(z_size)]
+            if i == 0:
+                pieces = [jnp.concatenate([piece, sum_rows], 0) for piece in pieces]
+            early.append(z_blocks(pieces, (0, 1)))
         sums = [
             jnp.sum(block[z_rows : z_rows + 3, :units].astype(f32), 0, keepdims=True)
-            for block in blocks
-        ]
-        blocks = [block[:z_rows] for block in blocks]
-        pre_early, mean_early, scale_early = finish_pre(blocks, sums)
-        grad_hidden_later = sum(block[:, :units].astype(f32) for block in blocks)
-        hidden = gelu_value(pre_early).astype(bf16)
-        hidden_early = z_gather(
-            jnp.concatenate([hidden, pack_side([mean_early, scale_early])], 1), (0,)
-        )
-        branch = t_scatter(matmul(hidden_early[:, :units], w_out_pair).astype(bf16))
-        middle_slab = (in_slab.astype(f32) + branch).astype(bf16)
-        middle_slab = pick(middle_slab, section_hop(middle_slab, 0))
-        middle = t_gather(middle_slab).reshape(half, pair_width)
+            for block in early[0]
+        ]
+        early[0] = [block[:z_rows] for block in early[0]]
+        early_norm = [finish_pre(blocks, sums) for blocks in early]
+        grad_hidden_later = [
+            sum(block[:, :units].astype(f32) for block in blocks) for blocks in early
+        ]
+        hidden_early = [
+            z_gather(
+                jnp.concatenate(
+                    [gelu_value(pre).astype(bf16), pack_side([mean, inv_scale])], 1
+                ),
+                (0,),
+            )
+            for pre, mean, inv_scale in early_norm
+        ]
+        middle_slab, middle = [], []
+        for i in streams:
+            branch = t_scatter(matmul(hidden_early[i][:, :units], w_out_pair).astype(bf16))
+            slab = (in_slab[i].astype(f32) + branch).astype(bf16)
+            slab = pick(slab, section_hop(slab, 0))
+            middle_slab.append(slab)
+            middle.append(t_gather(slab).reshape(half, pair_width))
 
     with jax.named_scope("tick1"):
-        blocks = z_scatter(forward_partial(middle), (1,))
-        pre_later, mean_later, scale_later = finish_pre(blocks, sums)
-        hidden_share = gelu_value(pre_later).astype(bf16)
-        grad_pre = (grad_hidden_later * gelu_slope(pre_later)).astype(bf16)
-        side = pack_side([mean_later, scale_later, *backward_sums(grad_pre, pre_later)])
-        grad_pre_later = z_gather(jnp.concatenate([grad_pre, side], 1), (1,))
-        partial = matmul_t(grad_pre_later[:, :units], w_in_pair).astype(bf16)
-        total = t_scatter(jnp.concatenate([partial, grad_pre_later[:, units:]], 1))
-        turn_slab = input_gradient(in_slab, total, middle_slab, grad_pre_later[:, units:])
-        turn_slab = pick(section_hop(turn_slab, 1), turn_slab)
-        turn = t_gather(turn_slab).reshape(half, pair_width)
+        hidden_share, grad_pre_later, turn_slab, turn = [], [], [], []
+        for i in streams:
+            blocks = z_scatter(forward_partial(middle[i]), (1,))
+            pre, mean, inv_scale = finish_pre(blocks, sums)
+            hidden_share.append(gelu_value(pre).astype(bf16))
+            grad_pre = (grad_hidden_later[i] * gelu_slope(pre)).astype(bf16)
+            side = pack_side([mean, inv_scale, *backward_sums(grad_pre, pre)])
+            grad_pre_later.append(z_gather(jnp.concatenate([grad_pre, side], 1), (1,)))
+        for i in streams:
+            side = grad_pre_later[i][:, units:]
+            partial = matmul_t(grad_pre_later[i][:, :units], w_in_pair).astype(bf16)
+            total = t_scatter(jnp.concatenate([partial, side], 1))
+            slab = input_gradient(in_slab[i], total, middle_slab[i], side)
+            slab = pick(section_hop(slab, 1), slab)
+            turn_slab.append(slab)
+            turn.append(t_gather(slab).reshape(half, pair_width))
 
     with jax.named_scope("tick2"):
-        blocks = z_scatter(matmul_t(turn, w_out_pair).astype(bf16), (0,))
-        grad_hidden = sum(block.astype(f32) for block in blocks)
-        grad_pre = (grad_hidden * gelu_slope(pre_early)).astype(bf16)
-        side = pack_side([mean_early, scale_early, *backward_sums(grad_pre, pre_early)])
-        share = jnp.concatenate([pick(grad_pre, hidden_share), side], 1)
-        last = z_gather(share, (0, 1))
-        partial = pick(
-            matmul_t(last[:, :units], w_in_pair), matmul(last[:, :units], w_out_pair)
-        ).astype(bf16)
-        total = t_scatter(jnp.concatenate([partial, last[:, units:]], 1))
-        final_slab = pick(
-            input_gradient(turn_slab, total, in_slab, last[:, units:]),
-            (middle_slab.astype(f32) + total[:, :pair_width]).astype(bf16),
-        )
-        final = t_gather(own_columns(final_slab).reshape(2, t_rows, own_width))
-        final = jnp.swapaxes(final, 0, 1).reshape(rows, own_width)
+        last, totals = [], []
+        for i in streams:
+            blocks = z_scatter(matmul_t(turn[i], w_out_pair).astype(bf16), (0,))
+            grad_hidden = sum(block.astype(f32) for block in blocks)
+            pre, mean, inv_scale = early_norm[i]
+            grad_pre = (grad_hidden * gelu_slope(pre)).astype(bf16)
+            side = pack_side([mean, inv_scale, *backward_sums(grad_pre, pre)])
+            share = jnp.concatenate([pick(grad_pre, hidden_share[i]), side], 1)
+            last.append(z_gather(share, (0, 1)))
+        for i in streams:
+            partial = pick(
+                matmul_t(last[i][:, :units], w_in_pair), matmul(last[i][:, :units], w_out_pair)
+            ).astype(bf16)
+            totals.append(t_scatter(jnp.concatenate([partial, last[i][:, units:]], 1)))
 
     with jax.named_scope("weights"):
-        middle_own = own_columns(middle)
-        turn_own = own_columns(turn)
-        grad_pre_half = pick(last, grad_pre_later)
-        hidden_half = pick(hidden_early, last)
-        grad_pre_all = jnp.concatenate([grad_pre_half, core_swap(grad_pre_half)], 0)
-        hidden_all = jnp.concatenate([hidden_half, core_swap(hidden_half)], 0)
+        middle_own = [own_columns(block) for block in middle]
+        turn_own = [own_columns(block) for block in turn]
+
+        def both_halves(early_halves, later_halves):
+            halves = [pick(*pair) for pair in zip(early_halves, later_halves)]
+            return jnp.concatenate([x for h in halves for x in (h, core_swap(h))], 0)
+
+        grad_pre_all = both_halves(last, grad_pre_later)
+        hidden_all = both_halves(hidden_early, last)
         side = grad_pre_all[:, units:]
-        section_input = pick(in_own, middle_own).astype(f32)
+        own_input = jnp.concatenate(in_own, 0)
+        section_input = pick(own_input, jnp.concatenate(middle_own, 0)).astype(f32)
         normed = ((section_input - side_value(side, 0)) * side_value(side, 1)).astype(bf16)
-        grad_out = pick(turn_own, in_own)
+        grad_out = pick(jnp.concatenate(turn_own, 0), own_input)
+        grad_w_out = matmul_ta(hidden_all[:, :units], grad_out).astype(bf16)
         grad_w_in = matmul_ta(normed, grad_pre_all[:, :units]).astype(bf16)
-        grad_w_out = matmul_ta(hidden_all[:, :units], grad_out).astype(bf16)
+
+    with jax.named_scope("last"):
+        totals[-1], grad_w_out, normed = lax.optimization_barrier((totals[-1], grad_w_out, normed))
+        final = []
+        for i in streams:
+            slab = pick(
+                input_gradient(turn_slab[i], totals[i], in_slab[i], last[i][:, units:]),
+                (middle_slab[i].astype(f32) + totals[i][:, :pair_width]).astype(bf16),
+            )
+            pair = turn_axis(own_columns(slab).reshape(2, t_rows, own_width), 0, core)
+            final.append(t_gather(pair))
+        final[-1], grad_w_in = lax.optimization_barrier((final[-1], grad_w_in))
+        final = [
+            turn_z(x.reshape(2, 2, tensor_size // 4, 2, t_rows, own_width)).reshape(rows, own_width)
+            for x in final
+        ]
 
     shape = (1,) + tokens.shape
+    middle_out = jnp.concatenate([arrange_back(block) for block in middle_own], 0)
+    turn_out = jnp.concatenate([arrange_back(block) for block in turn_own], 0)
+    final_out = jnp.concatenate(final, 0)
     return (
-        reorder(pick(middle_own, final)).reshape(shape),
-        reorder(pick(final, turn_own)).reshape(shape),
+        pick(middle_out, final_out).reshape(shape),
+        pick(final_out, turn_out).reshape(shape),
         grad_w_in[None],
         grad_w_out[None],
     )

time: 293 us -> 269 us (0.918)
  blocking collectives: 60.9 us -> 35.4 us
  waiting for transfers between devices: 108 us -> 88.6 us
  starting transfers between devices: 72.9 us -> 81.3 us
  other arithmetic: 19.4 us -> 25.6 us
  matrix products: 19.8 us -> 24.8 us
    all_to_all x2 -> x1, blocking collectives: 45.7 us -> 20.4 us  [t_scatter(): parts = lax.all_to_all(blocks, 'tensor', 0, 0)]
    ppermute x8, starting transfers between devices: 8 us -> 29.1 us  [core_swap(): return lax.ppermute(block, 'dp', [(i, i ^ 1) for i in range(dp_size)])]
    ppermute x2, waiting for transfers between devices: 35.2 us -> 18.4 us  [section_hop(): return lax.ppermute(block, 'section', [(source, 1 - source)])]
    ppermute x18, starting transfers between devices: 45.3 us -> 28.9 us  [z_blocks(): lax.ppermute(blocks[step], EVERYWHERE, z_route(dp_size, tensor_size, sect...]
    ppermute x18, waiting for transfers between devices: 31.9 us -> 24.1 us  [z_blocks(): lax.ppermute(blocks[step], EVERYWHERE, z_route(dp_size, tensor_size, sect...]
    all_to_all x1 -> x2, waiting for transfers between devices: 14.6 us -> 22.1 us  [t_scatter(): parts = lax.all_to_all(blocks, 'tensor', 0, 0)]
    all_to_all x1 -> x2, starting transfers between devices: 7.2 us -> 11.9 us  [t_scatter(): parts = lax.all_to_all(blocks, 'tensor', 0, 0)]
    select_n x8 -> x11, other arithmetic: 0.8 us -> 5.34 us  [turn_axis(): jnp.where(bit == 1, high, low)]
  transfers between devices with their start and end apart: 31 -> 32, of which waited for: 16 -> 18; matrix products, arithmetic and copies ran while one was open for 5% -> 13% of each run, Pallas kernels for 0% -> 0%
where the time goes in v2:
time: 269 us; the launch traced here: 268 us
  waiting for transfers between devices  88.6 us (33%)
  starting transfers between devices  81.3 us (30%)
  blocking collectives  35.4 us (13%)
  other arithmetic  25.6 us (10%)
  matrix products  24.8 us (9%)
  local copies, waits for them, and re-layouts  10.3 us (4%)
    ppermute x8, starting transfers between devices, core_swap(): return lax.ppermute(block, 'dp', [(i, i ^ 1) for i in range(dp_size)])  29.1 us
    ppermute x18, starting transfers between devices, z_blocks(): lax.ppermute(blocks[step], EVERYWHERE, z_route(dp_size, tensor_size, sect...  28.9 us
    ppermute x18, waiting for transfers between devices, z_blocks(): lax.ppermute(blocks[step], EVERYWHERE, z_route(dp_size, tensor_size, sect...  24.1 us
    all_to_all x2, waiting for transfers between devices, t_gather(): return lax.all_to_all(copies, 'tensor', 0, 0)  22.2 us
    all_to_all x2, waiting for transfers between devices, t_scatter(): parts = lax.all_to_all(blocks, 'tensor', 0, 0)  22.1 us
    all_to_all x1, blocking collectives, t_scatter(): parts = lax.all_to_all(blocks, 'tensor', 0, 0)  20.4 us
    ppermute x2, waiting for transfers between devices, section_hop(): return lax.ppermute(block, 'section', [(source, 1 - source)])  18.4 us
    all_to_all x1, blocking collectives, t_gather(): return lax.all_to_all(copies, 'tensor', 0, 0)  15 us
  transfers between devices with their start and end apart: 32, of which 18 were waited for; matrix products, arithmetic and copies ran while one was open for 13% of the time, Pallas kernels for 0%

profile of v2, /device:TPU:1, one launch (start us, length us, event | category | flops | bytes accessed | tf_op | source)
XLA Modules:
  0.0 268.3 jit_solution(16110511762083557694)
XLA Ops:
  0.6 3.3 %collective-permute-start.1 = (bf16[1024,896]{1,0:T(8,128)(2,1)}, bf16[1024,896]{1,0:T(8,128)(2,1)}, u32[]{:S(2)}, u32[]{:S(2)}) collective-permute-start(bf16[1024,896]{1,0:T(8,128)(2,1)} %bitcast.55), channel_id=1, source_target_pairs={{0,16},{16,0},{32,48},{48,32},{64,80},{80,64},{96,112},{112,96},{1... | collective-permute-start | bytes 5505032 | tf_op jit(solution)/shard_map/tick0/ppermute | solution.py:97
  15.3 5.3 %collective-permute-start.4 = (bf16[80,1024]{1,0:T(8,128)(2,1)S(1)}, bf16[80,1024]{1,0:T(8,128)(2,1)S(1)}, u32[]{:S(2)}, u32[]{:S(2)}) collective-permute-start(bf16[80,1024]{1,0:T(8,128)(2,1)S(1)} %get-tuple-element.121), channel_id=1, source_target_pairs={{0,64},{1,65},{2,66},{3,67},{4,68},{5,69},{6,70},{7,71},{8,72},{9,... | collective-permute-start | bytes 491528 | tf_op jit(solution)/shard_map/tick0/ppermute | solution.py:124
  24.7 11.6 %collective-permute-done.3 = bf16[80,1024]{1,0:T(8,128)(2,1)S(1)} collective-permute-done((bf16[80,1024]{1,0:T(8,128)(2,1)S(1)}, bf16[80,1024]{1,0:T(8,128)(2,1)S(1)}, u32[]{:S(2)}, u32[]{:S(2)}) %collective-permute-start.3) | collective-permute-done | bytes 163872 | tf_op jit(solution)/shard_map/tick0/ppermute | solution.py:124
  37.4 3.4 %collective-permute-start.8 = (bf16[64,1024]{1,0:T(8,128)(2,1)S(1)}, bf16[64,1024]{1,0:T(8,128)(2,1)}, u32[]{:S(2)}, u32[]{:S(2)}) collective-permute-start(bf16[64,1024]{1,0:T(8,128)(2,1)S(1)} %pad_maximum_fusion.25), channel_id=1, source_target_pairs={{0,96},{1,97},{2,98},{3,99},{4,100},{5,101},{6,102},{7,103},{8,104... | collective-permute-start | bytes 393224 | tf_op jit(solution)/shard_map/tick0/ppermute | solution.py:124
  44.2 6.5 %collective-permute-done.7 = bf16[64,1024]{1,0:T(8,128)(2,1)} collective-permute-done((bf16[64,1024]{1,0:T(8,128)(2,1)S(1)}, bf16[64,1024]{1,0:T(8,128)(2,1)}, u32[]{:S(2)}, u32[]{:S(2)}) %collective-permute-start.7) | collective-permute-done | bytes 131104 | tf_op jit(solution)/shard_map/tick0/ppermute | solution.py:124
  54.8 8.3 %all-to-all-start = ((bf16[16,16,2048]{2,1,0:T(8,128)(2,1)}), bf16[16,16,2048]{2,1,0:T(8,128)(2,1)S(1)}, u32[]{:S(2)}, u32[]{:S(2)}) async-start(bf16[16,16,2048]{2,1,0:T(8,128)(2,1)} %bitcast.61), calls=%async_computation | async-start | bytes 2097152 | tf_op jit(solution)/shard_map/tick0/all_to_all | solution.py:138
  63.0 14.7 %all-to-all-done = bf16[16,16,2048]{2,1,0:T(8,128)(2,1)S(1)} async-done(((bf16[16,16,2048]{2,1,0:T(8,128)(2,1)}), bf16[16,16,2048]{2,1,0:T(8,128)(2,1)S(1)}, u32[]{:S(2)}, u32[]{:S(2)}) %all-to-all-start) | async-done | bytes 1048608 | tf_op jit(solution)/shard_map/tick0/all_to_all | solution.py:138
  82.2 4.8 %all-to-all-start.1 = ((bf16[16,16,2048]{2,1,0:T(8,128)(2,1)}), bf16[16,16,2048]{2,1,0:T(8,128)(2,1)S(1)}, u32[]{:S(2)}, u32[]{:S(2)}) async-start(bf16[16,16,2048]{2,1,0:T(8,128)(2,1)} %broadcast_in_dim.537), calls=%async_computation.1 | async-start | bytes 2097152 | tf_op jit(solution)/shard_map/tick0/all_to_all | solution.py:143
  90.3 11.1 %all-to-all-done.1 = bf16[16,16,2048]{2,1,0:T(8,128)(2,1)S(1)} async-done(((bf16[16,16,2048]{2,1,0:T(8,128)(2,1)}), bf16[16,16,2048]{2,1,0:T(8,128)(2,1)S(1)}, u32[]{:S(2)}, u32[]{:S(2)}) %all-to-all-start.1) | async-done | bytes 1048608 | tf_op jit(solution)/shard_map/tick0/all_to_all | solution.py:143
  102.9 3.4 %fusion.4 = bf16[256,896]{1,0:T(8,128)(2,1)S(1)} fusion(bf16[256,2048]{1,0:T(8,128)(2,1)S(1)} %bitcast.32, f32[256]{0:T(256)} %broadcast_multiply_fusion, f32[896]{0:T(1024)} %copy-done.42, bf16[1024,896]{1,0:T(8,128)(2,1)} %collective-permute-done.1, bf16[1024,896]{1,0:T(8,128)(2,1)} %bitcast.56), kind=kOutput, calls=%fused_computation.22 | convolution fusion | flops 947552256 | bytes 5181952 | tf_op jit(solution)/shard_map/tick1/dot_general | solution.py:27
  106.5 3.8 %collective-permute-start.12 = (bf16[64,1024]{1,0:T(8,128)(2,1)S(1)}, bf16[64,1024]{1,0:T(8,128)(2,1)S(1)}, u32[]{:S(2)}, u32[]{:S(2)}) collective-permute-start(bf16[64,1024]{1,0:T(8,128)(2,1)S(1)} %get-tuple-element.110), channel_id=1, source_target_pairs={{0,16},{1,17},{2,18},{3,19},{4,20},{5,21},{6,22},{7,23},{8,24},{9,... | collective-permute-start | bytes 393224 | tf_op jit(solution)/shard_map/tick1/ppermute | solution.py:124
  117.8 20.4 %all_to_all.30 = bf16[16,16,2176]{2,1,0:T(8,128)(2,1)S(1)} all-to-all(bf16[16,16,2176]{2,1,0:T(8,128)(2,1)S(1)} %bitcast.40), channel_id=1, replica_groups=mesh['section'=2,'dp'=8,'tensor'=16] {'tensor'}, dimensions={0} | all-to-all | bytes 2228224 | tf_op jit(solution)/shard_map/tick1/all_to_all | solution.py:138
  140.2 17.1 %collective-permute-done.17 = bf16[16,2048]{1,0:T(8,128)(2,1)S(1)} collective-permute-done((bf16[16,2048]{1,0:T(8,128)(2,1)S(1)}, bf16[16,2048]{1,0:T(8,128)(2,1)S(1)}, u32[]{:S(2)}, u32[]{:S(2)}) %collective-permute-start.17) | collective-permute-done | bytes 65568 | tf_op jit(solution)/shard_map/tick1/ppermute | solution.py:100
  158.1 15.0 %all_to_all.31 = bf16[16,16,2048]{2,1,0:T(8,128)(2,1)S(1)} all-to-all(bf16[16,16,2048]{2,1,0:T(8,128)(2,1)S(1)} %broadcast_in_dim.563), channel_id=1, replica_groups=mesh['section'=2,'dp'=8,'tensor'=16] {'tensor'}, dimensions={0} | all-to-all | bytes 2097152 | tf_op jit(solution)/shard_map/tick1/all_to_all | solution.py:143
  174.5 4.3 %collective-permute-start.20 = (bf16[64,896]{1,0:T(8,128)(2,1)S(1)}, bf16[64,896]{1,0:T(8,128)(2,1)S(1)}, u32[]{:S(2)}, u32[]{:S(2)}) collective-permute-start(bf16[64,896]{1,0:T(8,128)(2,1)S(1)} %get-tuple-element.117), channel_id=1, source_target_pairs={{0,96},{1,97},{2,98},{3,99},{4,100},{5,101},{6,102},{7,103},{8,104... | collective-permute-start | bytes 344072 | tf_op jit(solution)/shard_map/tick2/ppermute | solution.py:124
  181.3 8.9 %collective-permute-start.10 = (bf16[256,1024]{1,0:T(8,128)(2,1)S(1)}, bf16[256,1024]{1,0:T(8,128)(2,1)S(1)}, u32[]{:S(2)}, u32[]{:S(2)}) collective-permute-start(bf16[256,1024]{1,0:T(8,128)(2,1)S(1)} %slice.335), channel_id=1, source_target_pairs={{0,16},{16,0},{32,48},{48,32},{64,80},{80,64},{96,112},{112,96},{1... | collective-permute-start | bytes 1572872 | tf_op jit(solution)/shard_map/weights/ppermute | solution.py:97
  198.9 8.9 %collective-permute-start.25 = (bf16[256,1024]{1,0:T(8,128)(2,1)}, bf16[256,1024]{1,0:T(8,128)(2,1)}, u32[]{:S(2)}, u32[]{:S(2)}) collective-permute-start(bf16[256,1024]{1,0:T(8,128)(2,1)} %slice.360), channel_id=1, source_target_pairs={{0,16},{16,0},{32,48},{48,32},{64,80},{80,64},{96,112},{112,96},{1... | collective-permute-start | bytes 1572872 | tf_op jit(solution)/shard_map/weights/ppermute | solution.py:97
  208.0 5.3 %collective-permute-start.26 = (bf16[256,1024]{1,0:T(8,128)(2,1)S(1)}, bf16[256,1024]{1,0:T(8,128)(2,1)}, u32[]{:S(2)}, u32[]{:S(2)}) collective-permute-start(bf16[256,1024]{1,0:T(8,128)(2,1)S(1)} %get-tuple-element.108), channel_id=1, source_target_pairs={{0,16},{16,0},{32,48},{48,32},{64,80},{80,64},{96,112},{112,96},{1... | collective-permute-start | bytes 1572872 | tf_op jit(solution)/shard_map/weights/ppermute | solution.py:97
  218.5 3.7 %all-to-all-start.4 = ((bf16[16,16,2176]{2,1,0:T(8,128)(2,1)}), bf16[16,16,2176]{2,1,0:T(8,128)(2,1)S(1)}, u32[]{:S(2)}, u32[]{:S(2)}) async-start(bf16[16,16,2176]{2,1,0:T(8,128)(2,1)} %bitcast.12), calls=%async_computation.4 | async-start | bytes 2228224 | tf_op jit(solution)/shard_map/tick2/all_to_all | solution.py:138
  228.8 3.5 %convolution_convert_fusion.3 = bf16[896,1024]{1,0:T(8,128)(2,1)} fusion(bf16[512,1024]{1,0:T(8,128)(2,1)S(1)} %bitcast.44, bf16[256,1024]{1,0:T(8,128)(2,1)} %collective-permute-done.25, bf16[256,1024]{1,0:T(8,128)(2,1)S(1)} %get-tuple-element.88, pred[]{:T(512)S(6)} %eq.293, bf16[256,1024]{1,0:T(8,128)(2,1)S(1)} %collective-permute-done.24, ...), kind=kOutput, calls=%fused_computation.18 | convolution fusion | flops 944898048 | bytes 4980737 | tf_op jit(solution)/shard_map/weights/dot_general | solution.py:35
  232.3 7.5 %all-to-all-done.4 = bf16[16,16,2176]{2,1,0:T(8,128)(2,1)S(1)} async-done(((bf16[16,16,2176]{2,1,0:T(8,128)(2,1)}), bf16[16,16,2176]{2,1,0:T(8,128)(2,1)S(1)}, u32[]{:S(2)}, u32[]{:S(2)}) %all-to-all-start.4) | async-done | bytes 1114144 | tf_op jit(solution)/shard_map/tick2/all_to_all | solution.py:138
  244.3 3.7 %all-to-all-start.5 = ((bf16[16,2,16,1024]{3,2,1,0:T(8,128)(2,1)}), bf16[16,2,16,1024]{3,2,1,0:T(8,128)(2,1)S(1)}, u32[]{:S(2)}, u32[]{:S(2)}) async-start(bf16[16,2,16,1024]{3,2,1,0:T(8,128)(2,1)} %broadcast_in_dim.571), calls=%async_computation.5 | async-start | bytes 2097152 | tf_op jit(solution)/shard_map/last/all_to_all | solution.py:143
  249.9 3.5 %convolution_convert_fusion.2 = bf16[1024,896]{1,0:T(8,128)(2,1)} fusion(bf16[512,1024]{1,0:T(8,128)(2,1)S(1)} %copy-done.14, bf16[256,1024]{1,0:T(8,128)(2,1)} %collective-permute-done.26, bf16[256,1024]{1,0:T(8,128)(2,1)S(1)} %get-tuple-element.108), kind=kOutput, calls=%fused_computation.17 | convolution fusion | flops 942276608 | bytes 3932160 | tf_op jit(solution)/shard_map/weights/dot_general | solution.py:35
  253.5 11.1 %all-to-all-done.5 = bf16[16,2,16,1024]{3,2,1,0:T(8,128)(2,1)S(1)} async-done(((bf16[16,2,16,1024]{3,2,1,0:T(8,128)(2,1)}), bf16[16,2,16,1024]{3,2,1,0:T(8,128)(2,1)S(1)}, u32[]{:S(2)}, u32[]{:S(2)}) %all-to-all-start.5) | async-done | bytes 1048608 | tf_op jit(solution)/shard_map/last/all_to_all | solution.py:143
  (357 shorter events, 77.0 us)
Async XLA Ops:
  0.6 8.2 %collective-permute-start.1 = (bf16[1024,896]{1,0:T(8,128)(2,1)}, bf16[1024,896]{1,0:T(8,128)(2,1)}, u32[]{:S(2)}, u32[]{:S(2)}) collective-permute-start(bf16[1024,896]{1,0:T(8,128)(2,1)} %bitcast.55), channel_id=1, source_target_pairs={{0,16},{16,0},{32,48},{48,32},{64,80},{80,64},{96,112},{112,96},{1... | collective-permute-start | bytes 5505032 | tf_op jit(solution)/shard_map/tick0/ppermute | solution.py:97
  7.0 6.7 %collective-permute-start.2 = (bf16[896,1024]{1,0:T(8,128)(2,1)S(1)}, bf16[896,1024]{1,0:T(8,128)(2,1)S(1)}, u32[]{:S(2)}, u32[]{:S(2)}) collective-permute-start(bf16[896,1024]{1,0:T(8,128)(2,1)S(1)} %bitcast.64), channel_id=1, source_target_pairs={{0,16},{16,0},{32,48},{48,32},{64,80},{80,64},{96,112},{112,96},{1... | collective-permute-start | bytes 5505032 | tf_op jit(solution)/shard_map/tick0/ppermute | solution.py:97
  15.3 9.4 %collective-permute-start.4 = (bf16[80,1024]{1,0:T(8,128)(2,1)S(1)}, bf16[80,1024]{1,0:T(8,128)(2,1)S(1)}, u32[]{:S(2)}, u32[]{:S(2)}) collective-permute-start(bf16[80,1024]{1,0:T(8,128)(2,1)S(1)} %get-tuple-element.121), channel_id=1, source_target_pairs={{0,64},{1,65},{2,66},{3,67},{4,68},{5,69},{6,70},{7,71},{8,72},{9,... | collective-permute-start | bytes 491528 | tf_op jit(solution)/shard_map/tick0/ppermute | solution.py:124
  20.6 15.7 %collective-permute-start.3 = (bf16[80,1024]{1,0:T(8,128)(2,1)S(1)}, bf16[80,1024]{1,0:T(8,128)(2,1)S(1)}, u32[]{:S(2)}, u32[]{:S(2)}) collective-permute-start(bf16[80,1024]{1,0:T(8,128)(2,1)S(1)} %get-tuple-element.122), channel_id=1, source_target_pairs={{0,32},{1,33},{2,34},{3,35},{4,36},{5,37},{6,38},{7,39},{8,40},{9,... | collective-permute-start | bytes 491528 | tf_op jit(solution)/shard_map/tick0/ppermute | solution.py:124
  21.8 14.6 %collective-permute-start.5 = (bf16[80,1024]{1,0:T(8,128)(2,1)S(1)}, bf16[80,1024]{1,0:T(8,128)(2,1)S(1)}, u32[]{:S(2)}, u32[]{:S(2)}) collective-permute-start(bf16[80,1024]{1,0:T(8,128)(2,1)S(1)} %get-tuple-element.123), channel_id=1, source_target_pairs={{0,96},{1,97},{2,98},{3,99},{4,100},{5,101},{6,102},{7,103},{8,104... | collective-permute-start | bytes 491528 | tf_op jit(solution)/shard_map/tick0/ppermute | solution.py:124
  37.4 6.8 %collective-permute-start.8 = (bf16[64,1024]{1,0:T(8,128)(2,1)S(1)}, bf16[64,1024]{1,0:T(8,128)(2,1)}, u32[]{:S(2)}, u32[]{:S(2)}) collective-permute-start(bf16[64,1024]{1,0:T(8,128)(2,1)S(1)} %pad_maximum_fusion.25), channel_id=1, source_target_pairs={{0,96},{1,97},{2,98},{3,99},{4,100},{5,101},{6,102},{7,103},{8,104... | collective-permute-start | bytes 393224 | tf_op jit(solution)/shard_map/tick0/ppermute | solution.py:124
  40.8 9.9 %collective-permute-start.7 = (bf16[64,1024]{1,0:T(8,128)(2,1)S(1)}, bf16[64,1024]{1,0:T(8,128)(2,1)}, u32[]{:S(2)}, u32[]{:S(2)}) collective-permute-start(bf16[64,1024]{1,0:T(8,128)(2,1)S(1)} %pad_maximum_fusion.25), channel_id=1, source_target_pairs={{0,64},{1,65},{2,66},{3,67},{4,68},{5,69},{6,70},{7,71},{8,72},{9,... | collective-permute-start | bytes 393224 | tf_op jit(solution)/shard_map/tick0/ppermute | solution.py:124
  41.3 9.5 %collective-permute-start.6 = (bf16[64,1024]{1,0:T(8,128)(2,1)S(1)}, bf16[64,1024]{1,0:T(8,128)(2,1)S(1)}, u32[]{:S(2)}, u32[]{:S(2)}) collective-permute-start(bf16[64,1024]{1,0:T(8,128)(2,1)S(1)} %pad_maximum_fusion.25), channel_id=1, source_target_pairs={{0,32},{1,33},{2,34},{3,35},{4,36},{5,37},{6,38},{7,39},{8,40},{9,... | collective-permute-start | bytes 393224 | tf_op jit(solution)/shard_map/tick0/ppermute | solution.py:124
  54.8 22.9 %all-to-all-start = ((bf16[16,16,2048]{2,1,0:T(8,128)(2,1)}), bf16[16,16,2048]{2,1,0:T(8,128)(2,1)S(1)}, u32[]{:S(2)}, u32[]{:S(2)}) async-start(bf16[16,16,2048]{2,1,0:T(8,128)(2,1)} %bitcast.61), calls=%async_computation | async-start | bytes 2097152 | tf_op jit(solution)/shard_map/tick0/all_to_all | solution.py:138
  82.2 19.1 %all-to-all-start.1 = ((bf16[16,16,2048]{2,1,0:T(8,128)(2,1)}), bf16[16,16,2048]{2,1,0:T(8,128)(2,1)S(1)}, u32[]{:S(2)}, u32[]{:S(2)}) async-start(bf16[16,16,2048]{2,1,0:T(8,128)(2,1)} %broadcast_in_dim.537), calls=%async_computation.1 | async-start | bytes 2097152 | tf_op jit(solution)/shard_map/tick0/all_to_all | solution.py:143
  106.5 4.8 %collective-permute-start.12 = (bf16[64,1024]{1,0:T(8,128)(2,1)S(1)}, bf16[64,1024]{1,0:T(8,128)(2,1)S(1)}, u32[]{:S(2)}, u32[]{:S(2)}) collective-permute-start(bf16[64,1024]{1,0:T(8,128)(2,1)S(1)} %get-tuple-element.110), channel_id=1, source_target_pairs={{0,16},{1,17},{2,18},{3,19},{4,20},{5,21},{6,22},{7,23},{8,24},{9,... | collective-permute-start | bytes 393224 | tf_op jit(solution)/shard_map/tick1/ppermute | solution.py:124
  138.7 18.7 %collective-permute-start.17 = (bf16[16,2048]{1,0:T(8,128)(2,1)S(1)}, bf16[16,2048]{1,0:T(8,128)(2,1)S(1)}, u32[]{:S(2)}, u32[]{:S(2)}) collective-permute-start(bf16[16,2048]{1,0:T(8,128)(2,1)S(1)} %fusion.56), channel_id=1, source_target_pairs={{128,0},{129,1},{130,2},{131,3},{132,4},{133,5},{134,6},{135,7},{1... | collective-permute-start | bytes 196616 | tf_op jit(solution)/shard_map/tick1/ppermute | solution.py:100
  174.4 15.8 %collective-permute-start.18 = (bf16[64,896]{1,0:T(8,128)(2,1)S(1)}, bf16[64,896]{1,0:T(8,128)(2,1)S(1)}, u32[]{:S(2)}, u32[]{:S(2)}) collective-permute-start(bf16[64,896]{1,0:T(8,128)(2,1)S(1)} %get-tuple-element.116), channel_id=1, source_target_pairs={{0,32},{1,33},{2,34},{3,35},{4,36},{5,37},{6,38},{7,39},{8,40},{9,... | collective-permute-start | bytes 344072 | tf_op jit(solution)/shard_map/tick2/ppermute | solution.py:124
  174.5 15.7 %collective-permute-start.20 = (bf16[64,896]{1,0:T(8,128)(2,1)S(1)}, bf16[64,896]{1,0:T(8,128)(2,1)S(1)}, u32[]{:S(2)}, u32[]{:S(2)}) collective-permute-start(bf16[64,896]{1,0:T(8,128)(2,1)S(1)} %get-tuple-element.117), channel_id=1, source_target_pairs={{0,96},{1,97},{2,98},{3,99},{4,100},{5,101},{6,102},{7,103},{8,104... | collective-permute-start | bytes 344072 | tf_op jit(solution)/shard_map/tick2/ppermute | solution.py:124
  178.9 11.4 %collective-permute-start.19 = (bf16[64,896]{1,0:T(8,128)(2,1)S(1)}, bf16[64,896]{1,0:T(8,128)(2,1)S(1)}, u32[]{:S(2)}, u32[]{:S(2)}) collective-permute-start(bf16[64,896]{1,0:T(8,128)(2,1)S(1)} %get-tuple-element.118), channel_id=1, source_target_pairs={{0,64},{1,65},{2,66},{3,67},{4,68},{5,69},{6,70},{7,71},{8,72},{9,... | collective-permute-start | bytes 344072 | tf_op jit(solution)/shard_map/tick2/ppermute | solution.py:124
  181.3 15.4 %collective-permute-start.10 = (bf16[256,1024]{1,0:T(8,128)(2,1)S(1)}, bf16[256,1024]{1,0:T(8,128)(2,1)S(1)}, u32[]{:S(2)}, u32[]{:S(2)}) collective-permute-start(bf16[256,1024]{1,0:T(8,128)(2,1)S(1)} %slice.335), channel_id=1, source_target_pairs={{0,16},{16,0},{32,48},{48,32},{64,80},{80,64},{96,112},{112,96},{1... | collective-permute-start | bytes 1572872 | tf_op jit(solution)/shard_map/weights/ppermute | solution.py:97
  191.0 16.8 %collective-permute-start.23 = (bf16[64,1024]{1,0:T(8,128)(2,1)S(1)}, bf16[64,1024]{1,0:T(8,128)(2,1)S(1)}, u32[]{:S(2)}, u32[]{:S(2)}) collective-permute-start(bf16[64,1024]{1,0:T(8,128)(2,1)S(1)} %pad_maximum_fusion.27), channel_id=1, source_target_pairs={{0,96},{1,97},{2,98},{3,99},{4,100},{5,101},{6,102},{7,103},{8,104... | collective-permute-start | bytes 393224 | tf_op jit(solution)/shard_map/tick2/ppermute | solution.py:124
  192.3 15.4 %collective-permute-start.22 = (bf16[64,1024]{1,0:T(8,128)(2,1)S(1)}, bf16[64,1024]{1,0:T(8,128)(2,1)S(1)}, u32[]{:S(2)}, u32[]{:S(2)}) collective-permute-start(bf16[64,1024]{1,0:T(8,128)(2,1)S(1)} %pad_maximum_fusion.27), channel_id=1, source_target_pairs={{0,64},{1,65},{2,66},{3,67},{4,68},{5,69},{6,70},{7,71},{8,72},{9,... | collective-permute-start | bytes 393224 | tf_op jit(solution)/shard_map/tick2/ppermute | solution.py:124
  194.7 13.1 %collective-permute-start.21 = (bf16[64,1024]{1,0:T(8,128)(2,1)S(1)}, bf16[64,1024]{1,0:T(8,128)(2,1)S(1)}, u32[]{:S(2)}, u32[]{:S(2)}) collective-permute-start(bf16[64,1024]{1,0:T(8,128)(2,1)S(1)} %pad_maximum_fusion.27), channel_id=1, source_target_pairs={{0,32},{1,33},{2,34},{3,35},{4,36},{5,37},{6,38},{7,39},{8,40},{9,... | collective-permute-start | bytes 393224 | tf_op jit(solution)/shard_map/tick2/ppermute | solution.py:124
  198.9 25.1 %collective-permute-start.25 = (bf16[256,1024]{1,0:T(8,128)(2,1)}, bf16[256,1024]{1,0:T(8,128)(2,1)}, u32[]{:S(2)}, u32[]{:S(2)}) collective-permute-start(bf16[256,1024]{1,0:T(8,128)(2,1)} %slice.360), channel_id=1, source_target_pairs={{0,16},{16,0},{32,48},{48,32},{64,80},{80,64},{96,112},{112,96},{1... | collective-permute-start | bytes 1572872 | tf_op jit(solution)/shard_map/weights/ppermute | solution.py:97
  208.0 18.3 %collective-permute-start.26 = (bf16[256,1024]{1,0:T(8,128)(2,1)S(1)}, bf16[256,1024]{1,0:T(8,128)(2,1)}, u32[]{:S(2)}, u32[]{:S(2)}) collective-permute-start(bf16[256,1024]{1,0:T(8,128)(2,1)S(1)} %get-tuple-element.108), channel_id=1, source_target_pairs={{0,16},{16,0},{32,48},{48,32},{64,80},{80,64},{96,112},{112,96},{1... | collective-permute-start | bytes 1572872 | tf_op jit(solution)/shard_map/weights/ppermute | solution.py:97
  218.5 21.2 %all-to-all-start.4 = ((bf16[16,16,2176]{2,1,0:T(8,128)(2,1)}), bf16[16,16,2176]{2,1,0:T(8,128)(2,1)S(1)}, u32[]{:S(2)}, u32[]{:S(2)}) async-start(bf16[16,16,2176]{2,1,0:T(8,128)(2,1)} %bitcast.12), calls=%async_computation.4 | async-start | bytes 2228224 | tf_op jit(solution)/shard_map/tick2/all_to_all | solution.py:138
  223.5 5.2 %collective-permute-start.24 = (bf16[256,1024]{1,0:T(8,128)(2,1)S(1)}, bf16[256,1024]{1,0:T(8,128)(2,1)S(1)}, u32[]{:S(2)}, u32[]{:S(2)}) collective-permute-start(bf16[256,1024]{1,0:T(8,128)(2,1)S(1)} %broadcast_select_fusion.4), channel_id=1, source_target_pairs={{0,16},{16,0},{32,48},{48,32},{64,80},{80,64},{96,112},{112,96},{1... | collective-permute-start | bytes 1572872 | tf_op jit(solution)/shard_map/weights/ppermute | solution.py:97
  244.3 20.3 %all-to-all-start.5 = ((bf16[16,2,16,1024]{3,2,1,0:T(8,128)(2,1)}), bf16[16,2,16,1024]{3,2,1,0:T(8,128)(2,1)S(1)}, u32[]{:S(2)}, u32[]{:S(2)}) async-start(bf16[16,2,16,1024]{3,2,1,0:T(8,128)(2,1)} %broadcast_in_dim.571), calls=%async_computation.5 | async-start | bytes 2097152 | tf_op jit(solution)/shard_map/last/all_to_all | solution.py:143
  (103 other events, 1039.8 us)

commit v3 on v2

--- a/solution.py
+++ b/solution.py
@@ -1,5 +1,6 @@
 import jax
 import jax.numpy as jnp
+import numpy as np
 from jax import lax
 from jax.sharding import PartitionSpec as P
 
@@ -42,19 +43,22 @@
     return high, middle, rest - middle
 
 
+def lane_mask(first, count):
+    mask = np.zeros((1, LANES), np.float32)
+    mask[0, first : first + count] = 1.0
+    return mask
+
+
 def pack_side(columns):
-    lane = lax.broadcasted_iota(jnp.int32, (1, LANES), 1)
-    block = jnp.zeros((columns[0].shape[0], LANES), f32)
+    block = 0.0
     for number, column in enumerate(columns):
         for part_no, part in enumerate(three_parts(column)):
-            block = jnp.where(lane == 3 * number + part_no, part, block)
+            block = block + part * lane_mask(3 * number + part_no, 1)
     return block.astype(bf16)
 
 
 def side_value(block, number):
-    lane = lax.broadcasted_iota(jnp.int32, block.shape, block.ndim - 1)
-    kept = jnp.where(lane // 3 == number, block.astype(f32), 0.0)
-    return jnp.sum(kept, axis=-1, keepdims=True)
+    return jnp.sum(block.astype(f32) * lane_mask(3 * number, 3), axis=-1, keepdims=True)
 
 
 def z_route(dp_size, tensor_size, sections, step):
@@ -133,10 +137,11 @@
     def z_gather(block, sections):
         return jnp.concatenate(z_blocks([block] * z_size, sections), 0)
 
-    def t_scatter(block):
+    def t_scatter(block, *ready):
+        block, *ready = lax.optimization_barrier((block, *ready))
         blocks = block.reshape(tensor_size, t_rows, block.shape[1])
         parts = lax.all_to_all(blocks, "tensor", 0, 0)
-        return jnp.sum(parts.astype(f32), 0)
+        return jnp.sum(parts.astype(f32), 0), *ready
 
     def t_gather(block):
         copies = jnp.broadcast_to(block[None], (tensor_size,) + block.shape)
@@ -172,10 +177,12 @@
         second = jnp.sum(values * pre, 1, keepdims=True)
         return first, second
 
-    def input_gradient(grad_slab, total, input_slab, side):
+    def slab_norm(side):
+        return side_value(t_slab(side), 0), side_value(t_slab(side), 1)
+
+    def input_gradient(grad_slab, total, input_slab, mean, inv_scale):
         first = side_value(total[:, pair_width:], 2) / width
         second = side_value(total[:, pair_width:], 3) / width
-        mean, inv_scale = side_value(t_slab(side), 0), side_value(t_slab(side), 1)
         normed = (input_slab.astype(f32) - mean) * inv_scale
         return (
             grad_slab.astype(f32) + inv_scale * (total[:, :pair_width] - first - normed * second)
@@ -185,7 +192,7 @@
         w_in_own, w_out_own = w_in[0], w_out[0]
         w_in_pair = jnp.concatenate([w_in_own, core_swap(w_in_own)], 0)
         w_out_pair = jnp.concatenate([w_out_own, core_swap(w_out_own)], 1)
-        column_sum = jnp.sum(w_in_pair.astype(f32), 0, keepdims=True)
+        column_sum = matmul(jnp.ones((16, pair_width), bf16), w_in_pair)[:1]
         sum_rows = jnp.concatenate(
             list(three_parts(column_sum)) + [jnp.zeros((13, units), f32)], 0
         ).astype(bf16)
@@ -196,34 +203,46 @@
         in_slab = [t_slab(block) for block in in_half]
         early = []
         for i in streams:
-            grad_partial = matmul_t(in_half[i], w_out_pair).astype(bf16)
-            grad_partial = jnp.concatenate([grad_partial, jnp.zeros((half, LANES), bf16)], 1)
-            partial = pick(forward_partial(in_half[i]), grad_partial)
+            partial = forward_partial(in_half[i])
             pieces = [partial[k * z_rows : (k + 1) * z_rows] for k in range(z_size)]
             if i == 0:
                 pieces = [jnp.concatenate([piece, sum_rows], 0) for piece in pieces]
-            early.append(z_blocks(pieces, (0, 1)))
+            early.append(z_blocks(pieces, (0,)))
         sums = [
             jnp.sum(block[z_rows : z_rows + 3, :units].astype(f32), 0, keepdims=True)
             for block in early[0]
         ]
         early[0] = [block[:z_rows] for block in early[0]]
         early_norm = [finish_pre(blocks, sums) for blocks in early]
-        grad_hidden_later = [
-            sum(block[:, :units].astype(f32) for block in blocks) for blocks in early
-        ]
-        hidden_early = [
-            z_gather(
-                jnp.concatenate(
-                    [gelu_value(pre).astype(bf16), pack_side([mean, inv_scale])], 1
-                ),
-                (0,),
+        sum_tiles = units // LANES
+        sum_block = jnp.concatenate(
+            [part.reshape(sum_tiles, LANES) for part in three_parts(column_sum)]
+            + [jnp.zeros((z_rows - 3 * sum_tiles, LANES), f32)],
+            0,
+        ).astype(bf16)
+        hidden_early, grad_hidden_later = [], []
+        for i in streams:
+            pre, mean, inv_scale = early_norm[i]
+            share = jnp.concatenate(
+                [gelu_value(pre).astype(bf16), pack_side([mean, inv_scale])], 1
             )
-            for pre, mean, inv_scale in early_norm
-        ]
+            grads = matmul_t(in_half[i], w_out_pair).astype(bf16)
+            grads = [
+                jnp.concatenate([grads[k * z_rows : (k + 1) * z_rows], sum_block], 1)
+                for k in range(z_size)
+            ]
+            blocks = z_blocks([pick(share, block) for block in grads], (0, 1))
+            if i == 0:
+                sent = [block[: 3 * sum_tiles, units:].astype(f32) for block in blocks]
+                sent = [jnp.sum(x.reshape(3, sum_tiles, LANES), 0) for x in sent]
+                sums = [pick(a, x.reshape(1, units)) for a, x in zip(sums, sent)]
+            hidden_early.append(jnp.concatenate(blocks, 0))
+            grad_hidden_later.append(sum(block[:, :units].astype(f32) for block in blocks))
         middle_slab, middle = [], []
         for i in streams:
-            branch = t_scatter(matmul(hidden_early[i][:, :units], w_out_pair).astype(bf16))
+            branch, in_slab[i] = t_scatter(
+                matmul(hidden_early[i][:, :units], w_out_pair).astype(bf16), in_slab[i]
+            )
             slab = (in_slab[i].astype(f32) + branch).astype(bf16)
             slab = pick(slab, section_hop(slab, 0))
             middle_slab.append(slab)
@@ -241,14 +260,14 @@
         for i in streams:
             side = grad_pre_later[i][:, units:]
             partial = matmul_t(grad_pre_later[i][:, :units], w_in_pair).astype(bf16)
-            total = t_scatter(jnp.concatenate([partial, side], 1))
-            slab = input_gradient(in_slab[i], total, middle_slab[i], side)
+            total, *norm = t_scatter(jnp.concatenate([partial, side], 1), *slab_norm(side))
+            slab = input_gradient(in_slab[i], total, middle_slab[i], *norm)
             slab = pick(section_hop(slab, 1), slab)
             turn_slab.append(slab)
             turn.append(t_gather(slab).reshape(half, pair_width))
 
     with jax.named_scope("tick2"):
-        last, totals = [], []
+        last, totals, last_norm = [], [], []
         for i in streams:
             blocks = z_scatter(matmul_t(turn[i], w_out_pair).astype(bf16), (0,))
             grad_hidden = sum(block.astype(f32) for block in blocks)
@@ -261,7 +280,10 @@
             partial = pick(
                 matmul_t(last[i][:, :units], w_in_pair), matmul(last[i][:, :units], w_out_pair)
             ).astype(bf16)
-            totals.append(t_scatter(jnp.concatenate([partial, last[i][:, units:]], 1)))
+            side = last[i][:, units:]
+            total, *norm = t_scatter(jnp.concatenate([partial, side], 1), *slab_norm(side))
+            totals.append(total)
+            last_norm.append(norm)
 
     with jax.named_scope("weights"):
         middle_own = [own_columns(block) for block in middle]
@@ -286,7 +308,7 @@
         final = []
         for i in streams:
             slab = pick(
-                input_gradient(turn_slab[i], totals[i], in_slab[i], last[i][:, units:]),
+                input_gradient(turn_slab[i], totals[i], in_slab[i], *last_norm[i]),
                 (middle_slab[i].astype(f32) + totals[i][:, :pair_width]).astype(bf16),
             )
             pair = turn_axis(own_columns(slab).reshape(2, t_rows, own_width), 0, core)

time: 269 us -> 257 us (0.955)
  waiting for transfers between devices: 88.6 us -> 62.3 us
  blocking collectives: 35.4 us -> 54.7 us
  matrix products: 24.8 us -> 34.2 us
  other arithmetic: 25.6 us -> 20.8 us
  local copies, waits for them, and re-layouts: 10.3 us -> 5.53 us
  starting transfers between devices: 81.3 us -> 76.7 us
    all_to_all x1 -> x2, blocking collectives: 20.4 us -> 40 us  [t_scatter(): parts = lax.all_to_all(blocks, 'tensor', 0, 0)]
    all_to_all x2 -> x1, waiting for transfers between devices: 22.1 us -> 9.07 us  [t_scatter(): parts = lax.all_to_all(blocks, 'tensor', 0, 0)]
    ppermute x18, waiting for transfers between devices: 24.1 us -> 15.8 us  [z_blocks(): lax.ppermute(blocks[step], EVERYWHERE, z_route(dp_size, tensor_size, sect...]
    all_to_all x2 -> x1, starting transfers between devices: 11.9 us -> 3.7 us  [t_scatter(): parts = lax.all_to_all(blocks, 'tensor', 0, 0)]
    ppermute x2, waiting for transfers between devices: 18.4 us -> 12.1 us  [section_hop(): return lax.ppermute(block, 'section', [(source, 1 - source)])]
    dot_general x4 -> x5, matrix products: 9.61 us -> 14.9 us  [matmul(): return jnp.dot(a, b, preferred_element_type=f32)]
    dot_general x4, matrix products: 8.13 us -> 12.2 us  [matmul_t(): lax.dot_general(a, b, (((1,), (1,)), ((), ())), preferred_element_type=f32)]
    eq x12 -> x0, other arithmetic: 3.28 us -> none  [pack_side(): block = jnp.where(lane == 3 * number + part_no, part, block)]
  transfers between devices with their start and end apart: 32 -> 31, of which waited for: 18 -> 17; matrix products, arithmetic and copies ran while one was open for 13% -> 15% of each run, Pallas kernels for 0% -> 0%
where the time goes in v3:
time: 257 us; the launch traced here: 256 us
  starting transfers between devices  76.7 us (30%)
  waiting for transfers between devices  62.3 us (24%)
  blocking collectives  54.7 us (21%)
  matrix products  34.2 us (13%)
  other arithmetic  20.8 us (8%)
  local copies, waits for them, and re-layouts  5.53 us (2%)
    all_to_all x2, blocking collectives, t_scatter(): parts = lax.all_to_all(blocks, 'tensor', 0, 0)  40 us
    ppermute x18, starting transfers between devices, z_blocks(): lax.ppermute(blocks[step], EVERYWHERE, z_route(dp_size, tensor_size, sect...  31.6 us
    ppermute x8, starting transfers between devices, core_swap(): return lax.ppermute(block, 'dp', [(i, i ^ 1) for i in range(dp_size)])  31 us
    all_to_all x2, waiting for transfers between devices, t_gather(): return lax.all_to_all(copies, 'tensor', 0, 0)  22.1 us
    ppermute x18, waiting for transfers between devices, z_blocks(): lax.ppermute(blocks[step], EVERYWHERE, z_route(dp_size, tensor_size, sect...  15.8 us
    dot_general x5, matrix products, matmul(): return jnp.dot(a, b, preferred_element_type=f32)  14.9 us
    all_to_all x1, blocking collectives, t_gather(): return lax.all_to_all(copies, 'tensor', 0, 0)  14.7 us
    dot_general x4, matrix products, matmul_t(): lax.dot_general(a, b, (((1,), (1,)), ((), ())), preferred_element_type=f32)  12.2 us
  transfers between devices with their start and end apart: 31, of which 17 were waited for; matrix products, arithmetic and copies ran while one was open for 15% of the time, Pallas kernels for 0%

profile of v3, /device:TPU:1, one launch (start us, length us, event | category | flops | bytes accessed | tf_op | source)
XLA Modules:
  0.0 256.2 jit_solution(10115418720007003664)
XLA Ops:
  0.6 3.3 %collective-permute-start.1 = (bf16[1024,896]{1,0:T(8,128)(2,1)}, bf16[1024,896]{1,0:T(8,128)(2,1)}, u32[]{:S(2)}, u32[]{:S(2)}) collective-permute-start(bf16[1024,896]{1,0:T(8,128)(2,1)} %bitcast.95), channel_id=1, source_target_pairs={{0,16},{16,0},{32,48},{48,32},{64,80},{80,64},{96,112},{112,96},{1... | collective-permute-start | bytes 5505032 | tf_op jit(solution)/shard_map/tick0/ppermute | solution.py:101
  14.8 4.4 %collective-permute-start.4 = (bf16[80,1024]{1,0:T(8,128)(2,1)S(1)}, bf16[80,1024]{1,0:T(8,128)(2,1)S(1)}, u32[]{:S(2)}, u32[]{:S(2)}) collective-permute-start(bf16[80,1024]{1,0:T(8,128)(2,1)S(1)} %get-tuple-element.121), channel_id=1, source_target_pairs={{0,96},{1,97},{2,98},{3,99},{4,100},{5,101},{6,102},{7,103},{8,104... | collective-permute-start | bytes 491528 | tf_op jit(solution)/shard_map/tick0/ppermute | solution.py:128
  21.4 3.3 %convolution_convert_fusion.5 = bf16[256,896]{1,0:T(8,128)(2,1)S(1)} fusion(bf16[256,1024]{1,0:T(8,128)(2,1)S(1)} %collective-permute-done, bf16[256,1024]{1,0:T(8,128)(2,1)S(1)} %bitcast.68, bf16[896,1024]{1,0:T(8,128)(2,1)} %collective-permute-done.5, bf16[896,1024]{1,0:T(8,128)(2,1)} %bitcast.8), kind=kOutput, calls=%fused_computation.23 | convolution fusion | flops 949190656 | bytes 5177344 | tf_op jit(solution)/shard_map/tick0/dot_general | solution.py:32
  25.2 7.8 %collective-permute-done.3 = bf16[80,1024]{1,0:T(8,128)(2,1)S(1)} collective-permute-done((bf16[80,1024]{1,0:T(8,128)(2,1)S(1)}, bf16[80,1024]{1,0:T(8,128)(2,1)S(1)}, u32[]{:S(2)}, u32[]{:S(2)}) %collective-permute-start.3) | collective-permute-done | bytes 163872 | tf_op jit(solution)/shard_map/tick0/ppermute | solution.py:128
  40.2 4.2 %collective-permute-done.7 = bf16[64,1024]{1,0:T(8,128)(2,1)S(1)} collective-permute-done((bf16[64,1024]{1,0:T(8,128)(2,1)S(1)}, bf16[64,1024]{1,0:T(8,128)(2,1)S(1)}, u32[]{:S(2)}, u32[]{:S(2)}) %collective-permute-start.7) | collective-permute-done | bytes 131104 | tf_op jit(solution)/shard_map/tick0/ppermute | solution.py:128
  45.8 3.4 %convolution_convert_fusion.1 = bf16[256,2048]{1,0:T(8,128)(2,1)S(1)} fusion(bf16[256,1024]{1,0:T(8,128)(2,1)S(1)} %pad_maximum_fusion.18, bf16[896,1024]{1,0:T(8,128)(2,1)} %collective-permute-done.5, bf16[896,1024]{1,0:T(8,128)(2,1)} %bitcast.8), kind=kOutput, calls=%fused_computation.9 | convolution fusion | flops 947388416 | bytes 5177344 | tf_op jit(solution)/shard_map/tick0/dot_general | solution.py:28
  49.2 19.9 %all_to_all.30 = bf16[16,16,2048]{2,1,0:T(8,128)(2,1)S(1)} all-to-all(bf16[16,16,2048]{2,1,0:T(8,128)(2,1)S(1)} %bitcast.86), channel_id=1, replica_groups=mesh['section'=2,'dp'=8,'tensor'=16] {'tensor'}, dimensions={0} | all-to-all | bytes 2097152 | tf_op jit(solution)/shard_map/tick0/all_to_all | solution.py:143
  72.9 4.2 %all-to-all-start.1 = ((bf16[16,16,2048]{2,1,0:T(8,128)(2,1)}), bf16[16,16,2048]{2,1,0:T(8,128)(2,1)S(1)}, u32[]{:S(2)}, u32[]{:S(2)}) async-start(bf16[16,16,2048]{2,1,0:T(8,128)(2,1)} %broadcast_in_dim.27), calls=%async_computation.1 | async-start | bytes 2097152 | tf_op jit(solution)/shard_map/tick0/all_to_all | solution.py:148
  77.3 11.8 %all-to-all-done.1 = bf16[16,16,2048]{2,1,0:T(8,128)(2,1)S(1)} async-done(((bf16[16,16,2048]{2,1,0:T(8,128)(2,1)}), bf16[16,16,2048]{2,1,0:T(8,128)(2,1)S(1)}, u32[]{:S(2)}, u32[]{:S(2)}) %all-to-all-start.1) | async-done | bytes 1048608 | tf_op jit(solution)/shard_map/tick0/all_to_all | solution.py:148
  93.3 6.3 %collective-permute-start.13 = (bf16[64,1024]{1,0:T(8,128)(2,1)S(1)}, bf16[64,1024]{1,0:T(8,128)(2,1)S(1)}, u32[]{:S(2)}, u32[]{:S(2)}) collective-permute-start(bf16[64,1024]{1,0:T(8,128)(2,1)S(1)} %get-tuple-element.126), channel_id=1, source_target_pairs={{0,16},{1,17},{2,18},{3,19},{4,20},{5,21},{6,22},{7,23},{8,24},{9,... | collective-permute-start | bytes 393224 | tf_op jit(solution)/shard_map/tick1/ppermute | solution.py:128
  107.3 20.1 %all_to_all.31 = bf16[16,16,2176]{2,1,0:T(8,128)(2,1)S(1)} all-to-all(bf16[16,16,2176]{2,1,0:T(8,128)(2,1)S(1)} %bitcast.71), channel_id=1, replica_groups=mesh['section'=2,'dp'=8,'tensor'=16] {'tensor'}, dimensions={0} | all-to-all | bytes 2228224 | tf_op jit(solution)/shard_map/tick1/all_to_all | solution.py:143
  129.2 10.8 %collective-permute-done.17 = bf16[16,2048]{1,0:T(8,128)(2,1)S(1)} collective-permute-done((bf16[16,2048]{1,0:T(8,128)(2,1)S(1)}, bf16[16,2048]{1,0:T(8,128)(2,1)S(1)}, u32[]{:S(2)}, u32[]{:S(2)}) %collective-permute-start.17) | collective-permute-done | bytes 65568 | tf_op jit(solution)/shard_map/tick1/ppermute | solution.py:104
  140.1 14.7 %all_to_all.32 = bf16[16,16,2048]{2,1,0:T(8,128)(2,1)S(1)} all-to-all(bf16[16,16,2048]{2,1,0:T(8,128)(2,1)S(1)} %broadcast_in_dim.30), channel_id=1, replica_groups=mesh['section'=2,'dp'=8,'tensor'=16] {'tensor'}, dimensions={0} | all-to-all | bytes 2097152 | tf_op jit(solution)/shard_map/tick1/all_to_all | solution.py:148
  154.8 3.3 %convolution_convert_fusion.4 = bf16[256,896]{1,0:T(8,128)(2,1)S(1)} fusion(bf16[256,2048]{1,0:T(8,128)(2,1)S(1)} %bitcast.72, bf16[896,1024]{1,0:T(8,128)(2,1)} %collective-permute-done.5, bf16[896,1024]{1,0:T(8,128)(2,1)} %bitcast.8), kind=kOutput, calls=%fused_computation.22 | convolution fusion | flops 947093504 | bytes 5177344 | tf_op jit(solution)/shard_map/tick2/dot_general | solution.py:32
  159.8 4.2 %collective-permute-start.19 = (bf16[64,896]{1,0:T(8,128)(2,1)S(1)}, bf16[64,896]{1,0:T(8,128)(2,1)S(1)}, u32[]{:S(2)}, u32[]{:S(2)}) collective-permute-start(bf16[64,896]{1,0:T(8,128)(2,1)S(1)} %get-tuple-element.131), channel_id=1, source_target_pairs={{0,64},{1,65},{2,66},{3,67},{4,68},{5,69},{6,70},{7,71},{8,72},{9,... | collective-permute-start | bytes 344072 | tf_op jit(solution)/shard_map/tick2/ppermute | solution.py:128
  165.1 13.9 %collective-permute-start.10 = (bf16[256,1024]{1,0:T(8,128)(2,1)S(1)}, bf16[256,1024]{1,0:T(8,128)(2,1)S(1)}, u32[]{:S(2)}, u32[]{:S(2)}) collective-permute-start(bf16[256,1024]{1,0:T(8,128)(2,1)S(1)} %slice.387), channel_id=1, source_target_pairs={{0,16},{16,0},{32,48},{48,32},{64,80},{80,64},{96,112},{112,96},{1... | collective-permute-start | bytes 1572872 | tf_op jit(solution)/shard_map/weights/ppermute | solution.py:101
  187.6 7.9 %collective-permute-start.25 = (bf16[256,1024]{1,0:T(8,128)(2,1)}, bf16[256,1024]{1,0:T(8,128)(2,1)}, u32[]{:S(2)}, u32[]{:S(2)}) collective-permute-start(bf16[256,1024]{1,0:T(8,128)(2,1)} %slice.420), channel_id=1, source_target_pairs={{0,16},{16,0},{32,48},{48,32},{64,80},{80,64},{96,112},{112,96},{1... | collective-permute-start | bytes 1572872 | tf_op jit(solution)/shard_map/weights/ppermute | solution.py:101
  195.8 3.9 %collective-permute-start.26 = (bf16[256,1024]{1,0:T(8,128)(2,1)S(1)}, bf16[256,1024]{1,0:T(8,128)(2,1)}, u32[]{:S(2)}, u32[]{:S(2)}) collective-permute-start(bf16[256,1024]{1,0:T(8,128)(2,1)S(1)} %get-tuple-element.124), channel_id=1, source_target_pairs={{0,16},{16,0},{32,48},{48,32},{64,80},{80,64},{96,112},{112,96},{1... | collective-permute-start | bytes 1572872 | tf_op jit(solution)/shard_map/weights/ppermute | solution.py:101
  207.1 3.7 %all-to-all-start.4 = ((bf16[16,16,2176]{2,1,0:T(8,128)(2,1)}), bf16[16,16,2176]{2,1,0:T(8,128)(2,1)S(1)}, u32[]{:S(2)}, u32[]{:S(2)}) async-start(bf16[16,16,2176]{2,1,0:T(8,128)(2,1)} %bitcast.26), calls=%async_computation.4 | async-start | bytes 2228224 | tf_op jit(solution)/shard_map/tick2/all_to_all | solution.py:143
  217.0 3.5 %convolution_convert_fusion.3 = bf16[896,1024]{1,0:T(8,128)(2,1)} fusion(bf16[512,1024]{1,0:T(8,128)(2,1)S(1)} %bitcast.75, bf16[256,1024]{1,0:T(8,128)(2,1)} %collective-permute-done.25, bf16[256,1024]{1,0:T(8,128)(2,1)S(1)} %get-tuple-element.107, pred[]{:T(512)S(6)} %eq.14, bf16[256,1024]{1,0:T(8,128)(2,1)S(1)} %collective-permute-done.24, ...), kind=kOutput, calls=%fused_computation.17 | convolution fusion | flops 944898048 | bytes 4980737 | tf_op jit(solution)/shard_map/weights/dot_general | solution.py:36
  220.5 9.1 %all-to-all-done.4 = bf16[16,16,2176]{2,1,0:T(8,128)(2,1)S(1)} async-done(((bf16[16,16,2176]{2,1,0:T(8,128)(2,1)}), bf16[16,16,2176]{2,1,0:T(8,128)(2,1)S(1)}, u32[]{:S(2)}, u32[]{:S(2)}) %all-to-all-start.4) | async-done | bytes 1114144 | tf_op jit(solution)/shard_map/tick2/all_to_all | solution.py:143
  233.2 3.7 %all-to-all-start.5 = ((bf16[16,2,16,1024]{3,2,1,0:T(8,128)(2,1)}), bf16[16,2,16,1024]{3,2,1,0:T(8,128)(2,1)S(1)}, u32[]{:S(2)}, u32[]{:S(2)}) async-start(bf16[16,2,16,1024]{3,2,1,0:T(8,128)(2,1)} %broadcast_in_dim.33), calls=%async_computation.5 | async-start | bytes 2097152 | tf_op jit(solution)/shard_map/last/all_to_all | solution.py:148
  239.6 3.5 %convolution_convert_fusion.2 = bf16[1024,896]{1,0:T(8,128)(2,1)} fusion(bf16[512,1024]{1,0:T(8,128)(2,1)S(1)} %copy-done.20, bf16[256,1024]{1,0:T(8,128)(2,1)} %collective-permute-done.26, bf16[256,1024]{1,0:T(8,128)(2,1)S(1)} %get-tuple-element.124), kind=kOutput, calls=%fused_computation.16 | convolution fusion | flops 942276608 | bytes 3932160 | tf_op jit(solution)/shard_map/weights/dot_general | solution.py:36
  243.2 10.3 %all-to-all-done.5 = bf16[16,2,16,1024]{3,2,1,0:T(8,128)(2,1)S(1)} async-done(((bf16[16,2,16,1024]{3,2,1,0:T(8,128)(2,1)}), bf16[16,2,16,1024]{3,2,1,0:T(8,128)(2,1)S(1)}, u32[]{:S(2)}, u32[]{:S(2)}) %all-to-all-start.5) | async-done | bytes 1048608 | tf_op jit(solution)/shard_map/last/all_to_all | solution.py:148
  (258 shorter events, 72.8 us)
Async XLA Ops:
  0.6 9.1 %collective-permute-start.1 = (bf16[1024,896]{1,0:T(8,128)(2,1)}, bf16[1024,896]{1,0:T(8,128)(2,1)}, u32[]{:S(2)}, u32[]{:S(2)}) collective-permute-start(bf16[1024,896]{1,0:T(8,128)(2,1)} %bitcast.95), channel_id=1, source_target_pairs={{0,16},{16,0},{32,48},{48,32},{64,80},{80,64},{96,112},{112,96},{1... | collective-permute-start | bytes 5505032 | tf_op jit(solution)/shard_map/tick0/ppermute | solution.py:101
  5.7 3.2 %collective-permute-start = (bf16[256,1024]{1,0:T(8,128)(2,1)S(1)}, bf16[256,1024]{1,0:T(8,128)(2,1)S(1)}, u32[]{:S(2)}, u32[]{:S(2)}) collective-permute-start(bf16[256,1024]{1,0:T(8,128)(2,1)S(1)} %bitcast.84), channel_id=1, source_target_pairs={{0,16},{16,0},{32,48},{48,32},{64,80},{80,64},{96,112},{112,96},{1... | collective-permute-start | bytes 1572872 | tf_op jit(solution)/shard_map/tick0/ppermute | solution.py:101
  5.8 15.6 %collective-permute-start.5 = (bf16[896,1024]{1,0:T(8,128)(2,1)}, bf16[896,1024]{1,0:T(8,128)(2,1)}, u32[]{:S(2)}, u32[]{:S(2)}) collective-permute-start(bf16[896,1024]{1,0:T(8,128)(2,1)} %bitcast.8), channel_id=1, source_target_pairs={{0,16},{16,0},{32,48},{48,32},{64,80},{80,64},{96,112},{112,96},{1... | collective-permute-start | bytes 5505032 | tf_op jit(solution)/shard_map/tick0/ppermute | solution.py:101
  14.8 10.0 %collective-permute-start.4 = (bf16[80,1024]{1,0:T(8,128)(2,1)S(1)}, bf16[80,1024]{1,0:T(8,128)(2,1)S(1)}, u32[]{:S(2)}, u32[]{:S(2)}) collective-permute-start(bf16[80,1024]{1,0:T(8,128)(2,1)S(1)} %get-tuple-element.121), channel_id=1, source_target_pairs={{0,96},{1,97},{2,98},{3,99},{4,100},{5,101},{6,102},{7,103},{8,104... | collective-permute-start | bytes 491528 | tf_op jit(solution)/shard_map/tick0/ppermute | solution.py:128
  19.2 6.0 %collective-permute-start.2 = (bf16[80,1024]{1,0:T(8,128)(2,1)S(1)}, bf16[80,1024]{1,0:T(8,128)(2,1)S(1)}, u32[]{:S(2)}, u32[]{:S(2)}) collective-permute-start(bf16[80,1024]{1,0:T(8,128)(2,1)S(1)} %get-tuple-element.122), channel_id=1, source_target_pairs={{0,32},{1,33},{2,34},{3,35},{4,36},{5,37},{6,38},{7,39},{8,40},{9,... | collective-permute-start | bytes 491528 | tf_op jit(solution)/shard_map/tick0/ppermute | solution.py:128
  20.3 12.7 %collective-permute-start.3 = (bf16[80,1024]{1,0:T(8,128)(2,1)S(1)}, bf16[80,1024]{1,0:T(8,128)(2,1)S(1)}, u32[]{:S(2)}, u32[]{:S(2)}) collective-permute-start(bf16[80,1024]{1,0:T(8,128)(2,1)S(1)} %get-tuple-element.123), channel_id=1, source_target_pairs={{0,64},{1,65},{2,66},{3,67},{4,68},{5,69},{6,70},{7,71},{8,72},{9,... | collective-permute-start | bytes 491528 | tf_op jit(solution)/shard_map/tick0/ppermute | solution.py:128
  34.3 10.1 %collective-permute-start.7 = (bf16[64,1024]{1,0:T(8,128)(2,1)S(1)}, bf16[64,1024]{1,0:T(8,128)(2,1)S(1)}, u32[]{:S(2)}, u32[]{:S(2)}) collective-permute-start(bf16[64,1024]{1,0:T(8,128)(2,1)S(1)} %get-tuple-element.138), channel_id=1, source_target_pairs={{0,64},{1,65},{2,66},{3,67},{4,68},{5,69},{6,70},{7,71},{8,72},{9,... | collective-permute-start | bytes 393224 | tf_op jit(solution)/shard_map/tick0/ppermute | solution.py:128
  36.7 9.0 %collective-permute-start.8 = (bf16[64,1024]{1,0:T(8,128)(2,1)S(1)}, bf16[64,1024]{1,0:T(8,128)(2,1)S(1)}, u32[]{:S(2)}, u32[]{:S(2)}) collective-permute-start(bf16[64,1024]{1,0:T(8,128)(2,1)S(1)} %get-tuple-element.139), channel_id=1, source_target_pairs={{0,96},{1,97},{2,98},{3,99},{4,100},{5,101},{6,102},{7,103},{8,104... | collective-permute-start | bytes 393224 | tf_op jit(solution)/shard_map/tick0/ppermute | solution.py:128
  37.1 8.6 %collective-permute-start.6 = (bf16[64,1024]{1,0:T(8,128)(2,1)S(1)}, bf16[64,1024]{1,0:T(8,128)(2,1)S(1)}, u32[]{:S(2)}, u32[]{:S(2)}) collective-permute-start(bf16[64,1024]{1,0:T(8,128)(2,1)S(1)} %get-tuple-element.137), channel_id=1, source_target_pairs={{0,32},{1,33},{2,34},{3,35},{4,36},{5,37},{6,38},{7,39},{8,40},{9,... | collective-permute-start | bytes 393224 | tf_op jit(solution)/shard_map/tick0/ppermute | solution.py:128
  72.9 16.1 %all-to-all-start.1 = ((bf16[16,16,2048]{2,1,0:T(8,128)(2,1)}), bf16[16,16,2048]{2,1,0:T(8,128)(2,1)S(1)}, u32[]{:S(2)}, u32[]{:S(2)}) async-start(bf16[16,16,2048]{2,1,0:T(8,128)(2,1)} %broadcast_in_dim.27), calls=%async_computation.1 | async-start | bytes 2097152 | tf_op jit(solution)/shard_map/tick0/all_to_all | solution.py:148
  93.3 7.3 %collective-permute-start.13 = (bf16[64,1024]{1,0:T(8,128)(2,1)S(1)}, bf16[64,1024]{1,0:T(8,128)(2,1)S(1)}, u32[]{:S(2)}, u32[]{:S(2)}) collective-permute-start(bf16[64,1024]{1,0:T(8,128)(2,1)S(1)} %get-tuple-element.126), channel_id=1, source_target_pairs={{0,16},{1,17},{2,18},{3,19},{4,20},{5,21},{6,22},{7,23},{8,24},{9,... | collective-permute-start | bytes 393224 | tf_op jit(solution)/shard_map/tick1/ppermute | solution.py:128
  127.9 12.1 %collective-permute-start.17 = (bf16[16,2048]{1,0:T(8,128)(2,1)S(1)}, bf16[16,2048]{1,0:T(8,128)(2,1)S(1)}, u32[]{:S(2)}, u32[]{:S(2)}) collective-permute-start(bf16[16,2048]{1,0:T(8,128)(2,1)S(1)} %fusion.62), channel_id=1, source_target_pairs={{128,0},{129,1},{130,2},{131,3},{132,4},{133,5},{134,6},{135,7},{1... | collective-permute-start | bytes 196616 | tf_op jit(solution)/shard_map/tick1/ppermute | solution.py:104
  158.2 20.8 %collective-permute-start.18 = (bf16[64,896]{1,0:T(8,128)(2,1)S(1)}, bf16[64,896]{1,0:T(8,128)(2,1)S(1)}, u32[]{:S(2)}, u32[]{:S(2)}) collective-permute-start(bf16[64,896]{1,0:T(8,128)(2,1)S(1)} %get-tuple-element.129), channel_id=1, source_target_pairs={{0,32},{1,33},{2,34},{3,35},{4,36},{5,37},{6,38},{7,39},{8,40},{9,... | collective-permute-start | bytes 344072 | tf_op jit(solution)/shard_map/tick2/ppermute | solution.py:128
  158.3 20.7 %collective-permute-start.20 = (bf16[64,896]{1,0:T(8,128)(2,1)S(1)}, bf16[64,896]{1,0:T(8,128)(2,1)S(1)}, u32[]{:S(2)}, u32[]{:S(2)}) collective-permute-start(bf16[64,896]{1,0:T(8,128)(2,1)S(1)} %get-tuple-element.130), channel_id=1, source_target_pairs={{0,96},{1,97},{2,98},{3,99},{4,100},{5,101},{6,102},{7,103},{8,104... | collective-permute-start | bytes 344072 | tf_op jit(solution)/shard_map/tick2/ppermute | solution.py:128
  159.8 19.2 %collective-permute-start.19 = (bf16[64,896]{1,0:T(8,128)(2,1)S(1)}, bf16[64,896]{1,0:T(8,128)(2,1)S(1)}, u32[]{:S(2)}, u32[]{:S(2)}) collective-permute-start(bf16[64,896]{1,0:T(8,128)(2,1)S(1)} %get-tuple-element.131), channel_id=1, source_target_pairs={{0,64},{1,65},{2,66},{3,67},{4,68},{5,69},{6,70},{7,71},{8,72},{9,... | collective-permute-start | bytes 344072 | tf_op jit(solution)/shard_map/tick2/ppermute | solution.py:128
  165.1 20.4 %collective-permute-start.10 = (bf16[256,1024]{1,0:T(8,128)(2,1)S(1)}, bf16[256,1024]{1,0:T(8,128)(2,1)S(1)}, u32[]{:S(2)}, u32[]{:S(2)}) collective-permute-start(bf16[256,1024]{1,0:T(8,128)(2,1)S(1)} %slice.387), channel_id=1, source_target_pairs={{0,16},{16,0},{32,48},{48,32},{64,80},{80,64},{96,112},{112,96},{1... | collective-permute-start | bytes 1572872 | tf_op jit(solution)/shard_map/weights/ppermute | solution.py:101
  179.7 15.8 %collective-permute-start.23 = (bf16[64,1024]{1,0:T(8,128)(2,1)S(1)}, bf16[64,1024]{1,0:T(8,128)(2,1)S(1)}, u32[]{:S(2)}, u32[]{:S(2)}) collective-permute-start(bf16[64,1024]{1,0:T(8,128)(2,1)S(1)} %pad_maximum_fusion.29), channel_id=1, source_target_pairs={{0,96},{1,97},{2,98},{3,99},{4,100},{5,101},{6,102},{7,103},{8,104... | collective-permute-start | bytes 393224 | tf_op jit(solution)/shard_map/tick2/ppermute | solution.py:128
  181.7 13.9 %collective-permute-start.22 = (bf16[64,1024]{1,0:T(8,128)(2,1)S(1)}, bf16[64,1024]{1,0:T(8,128)(2,1)S(1)}, u32[]{:S(2)}, u32[]{:S(2)}) collective-permute-start(bf16[64,1024]{1,0:T(8,128)(2,1)S(1)} %pad_maximum_fusion.29), channel_id=1, source_target_pairs={{0,64},{1,65},{2,66},{3,67},{4,68},{5,69},{6,70},{7,71},{8,72},{9,... | collective-permute-start | bytes 393224 | tf_op jit(solution)/shard_map/tick2/ppermute | solution.py:128
  183.5 12.1 %collective-permute-start.21 = (bf16[64,1024]{1,0:T(8,128)(2,1)S(1)}, bf16[64,1024]{1,0:T(8,128)(2,1)S(1)}, u32[]{:S(2)}, u32[]{:S(2)}) collective-permute-start(bf16[64,1024]{1,0:T(8,128)(2,1)S(1)} %pad_maximum_fusion.29), channel_id=1, source_target_pairs={{0,32},{1,33},{2,34},{3,35},{4,36},{5,37},{6,38},{7,39},{8,40},{9,... | collective-permute-start | bytes 393224 | tf_op jit(solution)/shard_map/tick2/ppermute | solution.py:128
  187.6 24.6 %collective-permute-start.25 = (bf16[256,1024]{1,0:T(8,128)(2,1)}, bf16[256,1024]{1,0:T(8,128)(2,1)}, u32[]{:S(2)}, u32[]{:S(2)}) collective-permute-start(bf16[256,1024]{1,0:T(8,128)(2,1)} %slice.420), channel_id=1, source_target_pairs={{0,16},{16,0},{32,48},{48,32},{64,80},{80,64},{96,112},{112,96},{1... | collective-permute-start | bytes 1572872 | tf_op jit(solution)/shard_map/weights/ppermute | solution.py:101
  195.8 18.6 %collective-permute-start.26 = (bf16[256,1024]{1,0:T(8,128)(2,1)S(1)}, bf16[256,1024]{1,0:T(8,128)(2,1)}, u32[]{:S(2)}, u32[]{:S(2)}) collective-permute-start(bf16[256,1024]{1,0:T(8,128)(2,1)S(1)} %get-tuple-element.124), channel_id=1, source_target_pairs={{0,16},{16,0},{32,48},{48,32},{64,80},{80,64},{96,112},{112,96},{1... | collective-permute-start | bytes 1572872 | tf_op jit(solution)/shard_map/weights/ppermute | solution.py:101
  207.1 22.4 %all-to-all-start.4 = ((bf16[16,16,2176]{2,1,0:T(8,128)(2,1)}), bf16[16,16,2176]{2,1,0:T(8,128)(2,1)S(1)}, u32[]{:S(2)}, u32[]{:S(2)}) async-start(bf16[16,16,2176]{2,1,0:T(8,128)(2,1)} %bitcast.26), calls=%async_computation.4 | async-start | bytes 2228224 | tf_op jit(solution)/shard_map/tick2/all_to_all | solution.py:143
  212.1 4.9 %collective-permute-start.24 = (bf16[256,1024]{1,0:T(8,128)(2,1)S(1)}, bf16[256,1024]{1,0:T(8,128)(2,1)S(1)}, u32[]{:S(2)}, u32[]{:S(2)}) collective-permute-start(bf16[256,1024]{1,0:T(8,128)(2,1)S(1)} %broadcast_select_fusion.2), channel_id=1, source_target_pairs={{0,16},{16,0},{32,48},{48,32},{64,80},{80,64},{96,112},{112,96},{1... | collective-permute-start | bytes 1572872 | tf_op jit(solution)/shard_map/weights/ppermute | solution.py:101
  233.2 20.3 %all-to-all-start.5 = ((bf16[16,2,16,1024]{3,2,1,0:T(8,128)(2,1)}), bf16[16,2,16,1024]{3,2,1,0:T(8,128)(2,1)S(1)}, u32[]{:S(2)}, u32[]{:S(2)}) async-start(bf16[16,2,16,1024]{3,2,1,0:T(8,128)(2,1)} %broadcast_in_dim.33), calls=%async_computation.5 | async-start | bytes 2097152 | tf_op jit(solution)/shard_map/last/all_to_all | solution.py:148
  (56 other events, 669.7 us)

commit v4 on v3

--- a/solution.py
+++ b/solution.py
@@ -192,6 +192,8 @@
         w_in_own, w_out_own = w_in[0], w_out[0]
         w_in_pair = jnp.concatenate([w_in_own, core_swap(w_in_own)], 0)
         w_out_pair = jnp.concatenate([w_out_own, core_swap(w_out_own)], 1)
+        w_in_pair = lax.optimization_barrier(w_in_pair)
+        w_out_pair = lax.optimization_barrier(w_out_pair)
         column_sum = matmul(jnp.ones((16, pair_width), bf16), w_in_pair)[:1]
         sum_rows = jnp.concatenate(
             list(three_parts(column_sum)) + [jnp.zeros((13, units), f32)], 0

time: 257 us -> 247 us (0.961)
  matrix products: 34.2 us -> 19.9 us
  other arithmetic: 20.8 us -> 25 us
    dot_general x5, matrix products: 14.9 us -> 7.73 us  [matmul(): return jnp.dot(a, b, preferred_element_type=f32)]
    dot_general x4, matrix products: 12.2 us -> 5.14 us  [matmul_t(): lax.dot_general(a, b, (((1,), (1,)), ((), ())), preferred_element_type=f32)]
    concatenate x0 -> x2, other arithmetic: none -> 4.25 us  [the longest x1 2.46 us: body(): w_out_pair = jnp.concatenate([w_out_own, core_swap(w_out_own)], 1)]
  transfers between devices with their start and end apart: 31 -> 31, of which waited for: 17 -> 16; matrix products, arithmetic and copies ran while one was open for 15% -> 14% of each run, Pallas kernels for 0% -> 0%
where the time goes in v4:
time: 247 us; the launch traced here: 246 us
  starting transfers between devices  76.3 us (31%)
  waiting for transfers between devices  61.9 us (25%)
  blocking collectives  55.2 us (22%)
  other arithmetic  25 us (10%)
  matrix products  19.9 us (8%)
  local copies, waits for them, and re-layouts  5.62 us (2%)
    all_to_all x2, blocking collectives, t_scatter(): parts = lax.all_to_all(blocks, 'tensor', 0, 0)  40.5 us
    ppermute x18, starting transfers between devices, z_blocks(): lax.ppermute(blocks[step], EVERYWHERE, z_route(dp_size, tensor_size, sect...  31.5 us
    ppermute x8, starting transfers between devices, core_swap(): return lax.ppermute(block, 'dp', [(i, i ^ 1) for i in range(dp_size)])  30.5 us
    all_to_all x2, waiting for transfers between devices, t_gather(): return lax.all_to_all(copies, 'tensor', 0, 0)  22.2 us
    ppermute x18, waiting for transfers between devices, z_blocks(): lax.ppermute(blocks[step], EVERYWHERE, z_route(dp_size, tensor_size, sect...  15.3 us
    all_to_all x1, blocking collectives, t_gather(): return lax.all_to_all(copies, 'tensor', 0, 0)  14.7 us
    ppermute x2, waiting for transfers between devices, section_hop(): return lax.ppermute(block, 'section', [(source, 1 - source)])  12.1 us
    all_to_all x1, waiting for transfers between devices, t_scatter(): parts = lax.all_to_all(blocks, 'tensor', 0, 0)  9.05 us
  transfers between devices with their start and end apart: 31, of which 16 were waited for; matrix products, arithmetic and copies ran while one was open for 14% of the time, Pallas kernels for 0%

profile of v4, /device:TPU:1, one launch (start us, length us, event | category | flops | bytes accessed | tf_op | source)
XLA Modules:
  0.0 246.3 jit_solution(4685571709740564715)
XLA Ops:
  0.6 3.3 %collective-permute-start.1 = (bf16[1024,896]{1,0:T(8,128)(2,1)}, bf16[1024,896]{1,0:T(8,128)(2,1)}, u32[]{:S(2)}, u32[]{:S(2)}) collective-permute-start(bf16[1024,896]{1,0:T(8,128)(2,1)} %bitcast.95), channel_id=1, source_target_pairs={{0,16},{16,0},{32,48},{48,32},{64,80},{80,64},{96,112},{112,96},{1... | collective-permute-start | bytes 5505032 | tf_op jit(solution)/shard_map/tick0/ppermute | solution.py:101
  13.6 4.4 %collective-permute-start.4 = (bf16[80,1024]{1,0:T(8,128)(2,1)S(1)}, bf16[80,1024]{1,0:T(8,128)(2,1)S(1)}, u32[]{:S(2)}, u32[]{:S(2)}) collective-permute-start(bf16[80,1024]{1,0:T(8,128)(2,1)S(1)} %get-tuple-element.121), channel_id=1, source_target_pairs={{0,96},{1,97},{2,98},{3,99},{4,100},{5,101},{6,102},{7,103},{8,104... | collective-permute-start | bytes 491528 | tf_op jit(solution)/shard_map/tick0/ppermute | solution.py:128
  20.2 2.5 pad_maximum_fusion.1
  24.1 7.8 %collective-permute-done.3 = bf16[80,1024]{1,0:T(8,128)(2,1)S(1)} collective-permute-done((bf16[80,1024]{1,0:T(8,128)(2,1)S(1)}, bf16[80,1024]{1,0:T(8,128)(2,1)S(1)}, u32[]{:S(2)}, u32[]{:S(2)}) %collective-permute-start.3) | collective-permute-done | bytes 163872 | tf_op jit(solution)/shard_map/tick0/ppermute | solution.py:128
  36.0 3.1 %collective-permute-start.6 = (bf16[64,1024]{1,0:T(8,128)(2,1)S(1)}, bf16[64,1024]{1,0:T(8,128)(2,1)S(1)}, u32[]{:S(2)}, u32[]{:S(2)}) collective-permute-start(bf16[64,1024]{1,0:T(8,128)(2,1)S(1)} %get-tuple-element.137), channel_id=1, source_target_pairs={{0,32},{1,33},{2,34},{3,35},{4,36},{5,37},{6,38},{7,39},{8,40},{9,... | collective-permute-start | bytes 393224 | tf_op jit(solution)/shard_map/tick0/ppermute | solution.py:128
  39.1 4.1 %collective-permute-done.7 = bf16[64,1024]{1,0:T(8,128)(2,1)S(1)} collective-permute-done((bf16[64,1024]{1,0:T(8,128)(2,1)S(1)}, bf16[64,1024]{1,0:T(8,128)(2,1)S(1)}, u32[]{:S(2)}, u32[]{:S(2)}) %collective-permute-start.7) | collective-permute-done | bytes 131104 | tf_op jit(solution)/shard_map/tick0/ppermute | solution.py:128
  46.0 20.4 %all_to_all.30 = bf16[16,16,2048]{2,1,0:T(8,128)(2,1)S(1)} all-to-all(bf16[16,16,2048]{2,1,0:T(8,128)(2,1)S(1)} %bitcast.97), channel_id=1, replica_groups=mesh['section'=2,'dp'=8,'tensor'=16] {'tensor'}, dimensions={0} | all-to-all | bytes 2097152 | tf_op jit(solution)/shard_map/tick0/all_to_all | solution.py:143
  70.3 3.9 %all-to-all-start.1 = ((bf16[16,16,2048]{2,1,0:T(8,128)(2,1)}), bf16[16,16,2048]{2,1,0:T(8,128)(2,1)S(1)}, u32[]{:S(2)}, u32[]{:S(2)}) async-start(bf16[16,16,2048]{2,1,0:T(8,128)(2,1)} %broadcast_in_dim.27), calls=%async_computation.1 | async-start | bytes 2097152 | tf_op jit(solution)/shard_map/tick0/all_to_all | solution.py:148
  74.3 11.9 %all-to-all-done.1 = bf16[16,16,2048]{2,1,0:T(8,128)(2,1)S(1)} async-done(((bf16[16,16,2048]{2,1,0:T(8,128)(2,1)}), bf16[16,16,2048]{2,1,0:T(8,128)(2,1)S(1)}, u32[]{:S(2)}, u32[]{:S(2)}) %all-to-all-start.1) | async-done | bytes 1048608 | tf_op jit(solution)/shard_map/tick0/all_to_all | solution.py:148
  86.8 3.3 %fusion.4 = bf16[256,896]{1,0:T(8,128)(2,1)S(1)} fusion(bf16[256,2048]{1,0:T(8,128)(2,1)S(1)} %bitcast.72, bf16[2048,896]{1,0:T(8,128)(2,1)} %copy-done, f32[256]{0:T(256)S(1)} %get-tuple-element.148, f32[896]{0:T(1024)S(1)} %get-tuple-element.142), kind=kOutput, calls=%fused_computation.21 | convolution fusion | flops 940212224 | bytes 5181952 | tf_op jit(solution)/shard_map/tick1/dot_general | solution.py:28
  90.4 6.2 %collective-permute-start.13 = (bf16[64,1024]{1,0:T(8,128)(2,1)S(1)}, bf16[64,1024]{1,0:T(8,128)(2,1)S(1)}, u32[]{:S(2)}, u32[]{:S(2)}) collective-permute-start(bf16[64,1024]{1,0:T(8,128)(2,1)S(1)} %get-tuple-element.126), channel_id=1, source_target_pairs={{0,16},{1,17},{2,18},{3,19},{4,20},{5,21},{6,22},{7,23},{8,24},{9,... | collective-permute-start | bytes 393224 | tf_op jit(solution)/shard_map/tick1/ppermute | solution.py:128
  102.9 20.1 %all_to_all.31 = bf16[16,16,2176]{2,1,0:T(8,128)(2,1)S(1)} all-to-all(bf16[16,16,2176]{2,1,0:T(8,128)(2,1)S(1)} %bitcast.80), channel_id=1, replica_groups=mesh['section'=2,'dp'=8,'tensor'=16] {'tensor'}, dimensions={0} | all-to-all | bytes 2228224 | tf_op jit(solution)/shard_map/tick1/all_to_all | solution.py:143
  125.0 11.0 %collective-permute-done.17 = bf16[16,2048]{1,0:T(8,128)(2,1)S(1)} collective-permute-done((bf16[16,2048]{1,0:T(8,128)(2,1)S(1)}, bf16[16,2048]{1,0:T(8,128)(2,1)S(1)}, u32[]{:S(2)}, u32[]{:S(2)}) %collective-permute-start.17) | collective-permute-done | bytes 65568 | tf_op jit(solution)/shard_map/tick1/ppermute | solution.py:104
  136.1 14.7 %all_to_all.32 = bf16[16,16,2048]{2,1,0:T(8,128)(2,1)S(1)} all-to-all(bf16[16,16,2048]{2,1,0:T(8,128)(2,1)S(1)} %broadcast_in_dim.30), channel_id=1, replica_groups=mesh['section'=2,'dp'=8,'tensor'=16] {'tensor'}, dimensions={0} | all-to-all | bytes 2097152 | tf_op jit(solution)/shard_map/tick1/all_to_all | solution.py:148
  153.7 4.2 %collective-permute-start.19 = (bf16[64,896]{1,0:T(8,128)(2,1)S(1)}, bf16[64,896]{1,0:T(8,128)(2,1)S(1)}, u32[]{:S(2)}, u32[]{:S(2)}) collective-permute-start(bf16[64,896]{1,0:T(8,128)(2,1)S(1)} %get-tuple-element.131), channel_id=1, source_target_pairs={{0,64},{1,65},{2,66},{3,67},{4,68},{5,69},{6,70},{7,71},{8,72},{9,... | collective-permute-start | bytes 344072 | tf_op jit(solution)/shard_map/tick2/ppermute | solution.py:128
  159.1 13.4 %collective-permute-start.10 = (bf16[256,1024]{1,0:T(8,128)(2,1)S(1)}, bf16[256,1024]{1,0:T(8,128)(2,1)S(1)}, u32[]{:S(2)}, u32[]{:S(2)}) collective-permute-start(bf16[256,1024]{1,0:T(8,128)(2,1)S(1)} %slice.387), channel_id=1, source_target_pairs={{0,16},{16,0},{32,48},{48,32},{64,80},{80,64},{96,112},{112,96},{1... | collective-permute-start | bytes 1572872 | tf_op jit(solution)/shard_map/weights/ppermute | solution.py:101
  181.1 8.1 %collective-permute-start.25 = (bf16[256,1024]{1,0:T(8,128)(2,1)}, bf16[256,1024]{1,0:T(8,128)(2,1)}, u32[]{:S(2)}, u32[]{:S(2)}) collective-permute-start(bf16[256,1024]{1,0:T(8,128)(2,1)} %slice.420), channel_id=1, source_target_pairs={{0,16},{16,0},{32,48},{48,32},{64,80},{80,64},{96,112},{112,96},{1... | collective-permute-start | bytes 1572872 | tf_op jit(solution)/shard_map/weights/ppermute | solution.py:101
  192.2 3.8 %collective-permute-start.26 = (bf16[256,1024]{1,0:T(8,128)(2,1)S(1)}, bf16[256,1024]{1,0:T(8,128)(2,1)}, u32[]{:S(2)}, u32[]{:S(2)}) collective-permute-start(bf16[256,1024]{1,0:T(8,128)(2,1)S(1)} %get-tuple-element.124), channel_id=1, source_target_pairs={{0,16},{16,0},{32,48},{48,32},{64,80},{80,64},{96,112},{112,96},{1... | collective-permute-start | bytes 1572872 | tf_op jit(solution)/shard_map/weights/ppermute | solution.py:101
  197.2 3.7 %all-to-all-start.4 = ((bf16[16,16,2176]{2,1,0:T(8,128)(2,1)}), bf16[16,16,2176]{2,1,0:T(8,128)(2,1)S(1)}, u32[]{:S(2)}, u32[]{:S(2)}) async-start(bf16[16,16,2176]{2,1,0:T(8,128)(2,1)} %bitcast.26), calls=%async_computation.4 | async-start | bytes 2228224 | tf_op jit(solution)/shard_map/tick2/all_to_all | solution.py:143
  207.0 3.5 %convolution_convert_fusion.3 = bf16[896,1024]{1,0:T(8,128)(2,1)} fusion(bf16[512,1024]{1,0:T(8,128)(2,1)S(1)} %bitcast.84, bf16[256,1024]{1,0:T(8,128)(2,1)} %collective-permute-done.25, bf16[256,1024]{1,0:T(8,128)(2,1)S(1)} %get-tuple-element.107, pred[]{:T(512)S(6)} %eq.14, bf16[256,1024]{1,0:T(8,128)(2,1)S(1)} %collective-permute-done.24, ...), kind=kOutput, calls=%fused_computation.17 | convolution fusion | flops 944898048 | bytes 4980737 | tf_op jit(solution)/shard_map/weights/dot_general | solution.py:36
  210.6 9.0 %all-to-all-done.4 = bf16[16,16,2176]{2,1,0:T(8,128)(2,1)S(1)} async-done(((bf16[16,16,2176]{2,1,0:T(8,128)(2,1)}), bf16[16,16,2176]{2,1,0:T(8,128)(2,1)S(1)}, u32[]{:S(2)}, u32[]{:S(2)}) %all-to-all-start.4) | async-done | bytes 1114144 | tf_op jit(solution)/shard_map/tick2/all_to_all | solution.py:143
  223.3 3.7 %all-to-all-start.5 = ((bf16[16,2,16,1024]{3,2,1,0:T(8,128)(2,1)}), bf16[16,2,16,1024]{3,2,1,0:T(8,128)(2,1)S(1)}, u32[]{:S(2)}, u32[]{:S(2)}) async-start(bf16[16,2,16,1024]{3,2,1,0:T(8,128)(2,1)} %broadcast_in_dim.33), calls=%async_computation.5 | async-start | bytes 2097152 | tf_op jit(solution)/shard_map/last/all_to_all | solution.py:148
  229.7 3.5 %convolution_convert_fusion.2 = bf16[1024,896]{1,0:T(8,128)(2,1)} fusion(bf16[512,1024]{1,0:T(8,128)(2,1)S(1)} %copy-done.25, bf16[256,1024]{1,0:T(8,128)(2,1)} %collective-permute-done.26, bf16[256,1024]{1,0:T(8,128)(2,1)S(1)} %get-tuple-element.124), kind=kOutput, calls=%fused_computation.16 | convolution fusion | flops 942276608 | bytes 3932160 | tf_op jit(solution)/shard_map/weights/dot_general | solution.py:36
  233.3 10.3 %all-to-all-done.5 = bf16[16,2,16,1024]{3,2,1,0:T(8,128)(2,1)S(1)} async-done(((bf16[16,2,16,1024]{3,2,1,0:T(8,128)(2,1)}), bf16[16,2,16,1024]{3,2,1,0:T(8,128)(2,1)S(1)}, u32[]{:S(2)}, u32[]{:S(2)}) %all-to-all-start.5) | async-done | bytes 1048608 | tf_op jit(solution)/shard_map/last/all_to_all | solution.py:148
  (286 shorter events, 64.2 us)
Async XLA Ops:
  0.6 9.1 %collective-permute-start.1 = (bf16[1024,896]{1,0:T(8,128)(2,1)}, bf16[1024,896]{1,0:T(8,128)(2,1)}, u32[]{:S(2)}, u32[]{:S(2)}) collective-permute-start(bf16[1024,896]{1,0:T(8,128)(2,1)} %bitcast.95), channel_id=1, source_target_pairs={{0,16},{16,0},{32,48},{48,32},{64,80},{80,64},{96,112},{112,96},{1... | collective-permute-start | bytes 5505032 | tf_op jit(solution)/shard_map/tick0/ppermute | solution.py:101
  5.7 3.2 %collective-permute-start = (bf16[256,1024]{1,0:T(8,128)(2,1)S(1)}, bf16[256,1024]{1,0:T(8,128)(2,1)S(1)}, u32[]{:S(2)}, u32[]{:S(2)}) collective-permute-start(bf16[256,1024]{1,0:T(8,128)(2,1)S(1)} %bitcast.93), channel_id=1, source_target_pairs={{0,16},{16,0},{32,48},{48,32},{64,80},{80,64},{96,112},{112,96},{1... | collective-permute-start | bytes 1572872 | tf_op jit(solution)/shard_map/tick0/ppermute | solution.py:101
  5.8 14.4 %collective-permute-start.5 = (bf16[896,1024]{1,0:T(8,128)(2,1)}, bf16[896,1024]{1,0:T(8,128)(2,1)}, u32[]{:S(2)}, u32[]{:S(2)}) collective-permute-start(bf16[896,1024]{1,0:T(8,128)(2,1)} %bitcast.8), channel_id=1, source_target_pairs={{0,16},{16,0},{32,48},{48,32},{64,80},{80,64},{96,112},{112,96},{1... | collective-permute-start | bytes 5505032 | tf_op jit(solution)/shard_map/tick0/ppermute | solution.py:101
  13.6 10.4 %collective-permute-start.4 = (bf16[80,1024]{1,0:T(8,128)(2,1)S(1)}, bf16[80,1024]{1,0:T(8,128)(2,1)S(1)}, u32[]{:S(2)}, u32[]{:S(2)}) collective-permute-start(bf16[80,1024]{1,0:T(8,128)(2,1)S(1)} %get-tuple-element.121), channel_id=1, source_target_pairs={{0,96},{1,97},{2,98},{3,99},{4,100},{5,101},{6,102},{7,103},{8,104... | collective-permute-start | bytes 491528 | tf_op jit(solution)/shard_map/tick0/ppermute | solution.py:128
  18.0 6.1 %collective-permute-start.2 = (bf16[80,1024]{1,0:T(8,128)(2,1)S(1)}, bf16[80,1024]{1,0:T(8,128)(2,1)S(1)}, u32[]{:S(2)}, u32[]{:S(2)}) collective-permute-start(bf16[80,1024]{1,0:T(8,128)(2,1)S(1)} %get-tuple-element.122), channel_id=1, source_target_pairs={{0,32},{1,33},{2,34},{3,35},{4,36},{5,37},{6,38},{7,39},{8,40},{9,... | collective-permute-start | bytes 491528 | tf_op jit(solution)/shard_map/tick0/ppermute | solution.py:128
  19.2 12.7 %collective-permute-start.3 = (bf16[80,1024]{1,0:T(8,128)(2,1)S(1)}, bf16[80,1024]{1,0:T(8,128)(2,1)S(1)}, u32[]{:S(2)}, u32[]{:S(2)}) collective-permute-start(bf16[80,1024]{1,0:T(8,128)(2,1)S(1)} %get-tuple-element.123), channel_id=1, source_target_pairs={{0,64},{1,65},{2,66},{3,67},{4,68},{5,69},{6,70},{7,71},{8,72},{9,... | collective-permute-start | bytes 491528 | tf_op jit(solution)/shard_map/tick0/ppermute | solution.py:128
  33.2 10.0 %collective-permute-start.7 = (bf16[64,1024]{1,0:T(8,128)(2,1)S(1)}, bf16[64,1024]{1,0:T(8,128)(2,1)S(1)}, u32[]{:S(2)}, u32[]{:S(2)}) collective-permute-start(bf16[64,1024]{1,0:T(8,128)(2,1)S(1)} %get-tuple-element.138), channel_id=1, source_target_pairs={{0,64},{1,65},{2,66},{3,67},{4,68},{5,69},{6,70},{7,71},{8,72},{9,... | collective-permute-start | bytes 393224 | tf_op jit(solution)/shard_map/tick0/ppermute | solution.py:128
  35.6 9.1 %collective-permute-start.8 = (bf16[64,1024]{1,0:T(8,128)(2,1)S(1)}, bf16[64,1024]{1,0:T(8,128)(2,1)S(1)}, u32[]{:S(2)}, u32[]{:S(2)}) collective-permute-start(bf16[64,1024]{1,0:T(8,128)(2,1)S(1)} %get-tuple-element.139), channel_id=1, source_target_pairs={{0,96},{1,97},{2,98},{3,99},{4,100},{5,101},{6,102},{7,103},{8,104... | collective-permute-start | bytes 393224 | tf_op jit(solution)/shard_map/tick0/ppermute | solution.py:128
  36.0 8.6 %collective-permute-start.6 = (bf16[64,1024]{1,0:T(8,128)(2,1)S(1)}, bf16[64,1024]{1,0:T(8,128)(2,1)S(1)}, u32[]{:S(2)}, u32[]{:S(2)}) collective-permute-start(bf16[64,1024]{1,0:T(8,128)(2,1)S(1)} %get-tuple-element.137), channel_id=1, source_target_pairs={{0,32},{1,33},{2,34},{3,35},{4,36},{5,37},{6,38},{7,39},{8,40},{9,... | collective-permute-start | bytes 393224 | tf_op jit(solution)/shard_map/tick0/ppermute | solution.py:128
  70.3 15.9 %all-to-all-start.1 = ((bf16[16,16,2048]{2,1,0:T(8,128)(2,1)}), bf16[16,16,2048]{2,1,0:T(8,128)(2,1)S(1)}, u32[]{:S(2)}, u32[]{:S(2)}) async-start(bf16[16,16,2048]{2,1,0:T(8,128)(2,1)} %broadcast_in_dim.27), calls=%async_computation.1 | async-start | bytes 2097152 | tf_op jit(solution)/shard_map/tick0/all_to_all | solution.py:148
  90.4 7.2 %collective-permute-start.13 = (bf16[64,1024]{1,0:T(8,128)(2,1)S(1)}, bf16[64,1024]{1,0:T(8,128)(2,1)S(1)}, u32[]{:S(2)}, u32[]{:S(2)}) collective-permute-start(bf16[64,1024]{1,0:T(8,128)(2,1)S(1)} %get-tuple-element.126), channel_id=1, source_target_pairs={{0,16},{1,17},{2,18},{3,19},{4,20},{5,21},{6,22},{7,23},{8,24},{9,... | collective-permute-start | bytes 393224 | tf_op jit(solution)/shard_map/tick1/ppermute | solution.py:128
  123.5 12.5 %collective-permute-start.17 = (bf16[16,2048]{1,0:T(8,128)(2,1)S(1)}, bf16[16,2048]{1,0:T(8,128)(2,1)S(1)}, u32[]{:S(2)}, u32[]{:S(2)}) collective-permute-start(bf16[16,2048]{1,0:T(8,128)(2,1)S(1)} %fusion.62), channel_id=1, source_target_pairs={{128,0},{129,1},{130,2},{131,3},{132,4},{133,5},{134,6},{135,7},{1... | collective-permute-start | bytes 196616 | tf_op jit(solution)/shard_map/tick1/ppermute | solution.py:104
  152.2 20.3 %collective-permute-start.18 = (bf16[64,896]{1,0:T(8,128)(2,1)S(1)}, bf16[64,896]{1,0:T(8,128)(2,1)S(1)}, u32[]{:S(2)}, u32[]{:S(2)}) collective-permute-start(bf16[64,896]{1,0:T(8,128)(2,1)S(1)} %get-tuple-element.129), channel_id=1, source_target_pairs={{0,32},{1,33},{2,34},{3,35},{4,36},{5,37},{6,38},{7,39},{8,40},{9,... | collective-permute-start | bytes 344072 | tf_op jit(solution)/shard_map/tick2/ppermute | solution.py:128
  152.3 20.2 %collective-permute-start.20 = (bf16[64,896]{1,0:T(8,128)(2,1)S(1)}, bf16[64,896]{1,0:T(8,128)(2,1)S(1)}, u32[]{:S(2)}, u32[]{:S(2)}) collective-permute-start(bf16[64,896]{1,0:T(8,128)(2,1)S(1)} %get-tuple-element.130), channel_id=1, source_target_pairs={{0,96},{1,97},{2,98},{3,99},{4,100},{5,101},{6,102},{7,103},{8,104... | collective-permute-start | bytes 344072 | tf_op jit(solution)/shard_map/tick2/ppermute | solution.py:128
  153.7 18.8 %collective-permute-start.19 = (bf16[64,896]{1,0:T(8,128)(2,1)S(1)}, bf16[64,896]{1,0:T(8,128)(2,1)S(1)}, u32[]{:S(2)}, u32[]{:S(2)}) collective-permute-start(bf16[64,896]{1,0:T(8,128)(2,1)S(1)} %get-tuple-element.131), channel_id=1, source_target_pairs={{0,64},{1,65},{2,66},{3,67},{4,68},{5,69},{6,70},{7,71},{8,72},{9,... | collective-permute-start | bytes 344072 | tf_op jit(solution)/shard_map/tick2/ppermute | solution.py:128
  159.1 19.9 %collective-permute-start.10 = (bf16[256,1024]{1,0:T(8,128)(2,1)S(1)}, bf16[256,1024]{1,0:T(8,128)(2,1)S(1)}, u32[]{:S(2)}, u32[]{:S(2)}) collective-permute-start(bf16[256,1024]{1,0:T(8,128)(2,1)S(1)} %slice.387), channel_id=1, source_target_pairs={{0,16},{16,0},{32,48},{48,32},{64,80},{80,64},{96,112},{112,96},{1... | collective-permute-start | bytes 1572872 | tf_op jit(solution)/shard_map/weights/ppermute | solution.py:101
  173.2 16.1 %collective-permute-start.23 = (bf16[64,1024]{1,0:T(8,128)(2,1)S(1)}, bf16[64,1024]{1,0:T(8,128)(2,1)S(1)}, u32[]{:S(2)}, u32[]{:S(2)}) collective-permute-start(bf16[64,1024]{1,0:T(8,128)(2,1)S(1)} %pad_maximum_fusion.29), channel_id=1, source_target_pairs={{0,96},{1,97},{2,98},{3,99},{4,100},{5,101},{6,102},{7,103},{8,104... | collective-permute-start | bytes 393224 | tf_op jit(solution)/shard_map/tick2/ppermute | solution.py:128
  175.2 14.1 %collective-permute-start.22 = (bf16[64,1024]{1,0:T(8,128)(2,1)S(1)}, bf16[64,1024]{1,0:T(8,128)(2,1)S(1)}, u32[]{:S(2)}, u32[]{:S(2)}) collective-permute-start(bf16[64,1024]{1,0:T(8,128)(2,1)S(1)} %pad_maximum_fusion.29), channel_id=1, source_target_pairs={{0,64},{1,65},{2,66},{3,67},{4,68},{5,69},{6,70},{7,71},{8,72},{9,... | collective-permute-start | bytes 393224 | tf_op jit(solution)/shard_map/tick2/ppermute | solution.py:128
  177.1 12.2 %collective-permute-start.21 = (bf16[64,1024]{1,0:T(8,128)(2,1)S(1)}, bf16[64,1024]{1,0:T(8,128)(2,1)S(1)}, u32[]{:S(2)}, u32[]{:S(2)}) collective-permute-start(bf16[64,1024]{1,0:T(8,128)(2,1)S(1)} %pad_maximum_fusion.29), channel_id=1, source_target_pairs={{0,32},{1,33},{2,34},{3,35},{4,36},{5,37},{6,38},{7,39},{8,40},{9,... | collective-permute-start | bytes 393224 | tf_op jit(solution)/shard_map/tick2/ppermute | solution.py:128
  181.1 21.1 %collective-permute-start.25 = (bf16[256,1024]{1,0:T(8,128)(2,1)}, bf16[256,1024]{1,0:T(8,128)(2,1)}, u32[]{:S(2)}, u32[]{:S(2)}) collective-permute-start(bf16[256,1024]{1,0:T(8,128)(2,1)} %slice.420), channel_id=1, source_target_pairs={{0,16},{16,0},{32,48},{48,32},{64,80},{80,64},{96,112},{112,96},{1... | collective-permute-start | bytes 1572872 | tf_op jit(solution)/shard_map/weights/ppermute | solution.py:101
  192.2 12.3 %collective-permute-start.26 = (bf16[256,1024]{1,0:T(8,128)(2,1)S(1)}, bf16[256,1024]{1,0:T(8,128)(2,1)}, u32[]{:S(2)}, u32[]{:S(2)}) collective-permute-start(bf16[256,1024]{1,0:T(8,128)(2,1)S(1)} %get-tuple-element.124), channel_id=1, source_target_pairs={{0,16},{16,0},{32,48},{48,32},{64,80},{80,64},{96,112},{112,96},{1... | collective-permute-start | bytes 1572872 | tf_op jit(solution)/shard_map/weights/ppermute | solution.py:101
  197.2 22.4 %all-to-all-start.4 = ((bf16[16,16,2176]{2,1,0:T(8,128)(2,1)}), bf16[16,16,2176]{2,1,0:T(8,128)(2,1)S(1)}, u32[]{:S(2)}, u32[]{:S(2)}) async-start(bf16[16,16,2176]{2,1,0:T(8,128)(2,1)} %bitcast.26), calls=%async_computation.4 | async-start | bytes 2228224 | tf_op jit(solution)/shard_map/tick2/all_to_all | solution.py:143
  202.2 4.9 %collective-permute-start.24 = (bf16[256,1024]{1,0:T(8,128)(2,1)S(1)}, bf16[256,1024]{1,0:T(8,128)(2,1)S(1)}, u32[]{:S(2)}, u32[]{:S(2)}) collective-permute-start(bf16[256,1024]{1,0:T(8,128)(2,1)S(1)} %broadcast_select_fusion.2), channel_id=1, source_target_pairs={{0,16},{16,0},{32,48},{48,32},{64,80},{80,64},{96,112},{112,96},{1... | collective-permute-start | bytes 1572872 | tf_op jit(solution)/shard_map/weights/ppermute | solution.py:101
  223.3 20.3 %all-to-all-start.5 = ((bf16[16,2,16,1024]{3,2,1,0:T(8,128)(2,1)}), bf16[16,2,16,1024]{3,2,1,0:T(8,128)(2,1)S(1)}, u32[]{:S(2)}, u32[]{:S(2)}) async-start(bf16[16,2,16,1024]{3,2,1,0:T(8,128)(2,1)} %broadcast_in_dim.33), calls=%async_computation.5 | async-start | bytes 2097152 | tf_op jit(solution)/shard_map/last/all_to_all | solution.py:148
  (69 other events, 810.0 us)
